TPU v7x, 512 devices: a whole 4x8x8 slice. The times are simulated.
512 devices in a mesh: row: 32 (over y_lo, z), col: 16 (over y_hi, x, core).
Axes of the slice: x: 4, y: 8 (y_hi: 2, y_lo: 4; y = y_hi * 4 + y_lo), z: 8, core: 2. Of those that a mesh axis runs over, the one named last changes fastest.
Arguments:
- green: bfloat16 [128, 128, 4096], P('row', 'col'), may hold values from -4 to 4
- coupling: float32 [64], replicated, may hold values from 0.3 to 1
Outputs:
- collision: bfloat16 [128, 128, 4096], P('row', 'col')
- new_row: bfloat16 [128, 4096], P('col', 'row')
All inputs are finite; a program needn't handle non-finite values.
Results may differ from a plain program's by a relative error of at most 0.0046.
Values may be sent and summed in bfloat16 or wider, within the bound.
A program may use at most 64 MiB of HBM per device.

v0:
```python
import jax
import jax.numpy as jnp
from jax import lax
from jax.sharding import PartitionSpec as P

step_size = 0.01


def from_root(x, axis, root):
    mine = lax.axis_index(axis) == root
    return lax.psum(jnp.where(mine, x, jnp.zeros_like(x)), axis)


def shards(green, coupling):
    rows, cols, width = green.shape
    orbit = coupling.shape[0]
    n_row = lax.axis_size("row")
    total = rows * n_row
    spread = lax.all_to_all(green, "col", split_axis=2, concat_axis=1, tiled=True)
    landed = lax.all_to_all(
        lax.all_to_all(spread, "row", split_axis=1, concat_axis=0, tiled=True),
        "col",
        split_axis=0,
        concat_axis=2,
        tiled=True,
    )
    partner = jnp.transpose(
        landed.reshape(cols, rows, orbit, orbit).astype(jnp.float32), (1, 0, 3, 2)
    )
    own_block = green.reshape(rows, cols, orbit, orbit).astype(jnp.float32)
    pair = coupling[:, None] * coupling[None, :]
    sigma = (
        (pair * (own_block * own_block) * partner).astype(jnp.bfloat16).reshape(rows, cols, width)
    )
    sigma_all = lax.all_gather(sigma, "col", axis=1, tiled=True)
    first_times = lax.axis_index("row") * rows + jnp.arange(rows, dtype=jnp.int32)
    later_times = jnp.arange(total, dtype=jnp.int32)
    keep = later_times[None, :] <= first_times[:, None]
    sigma_all = jnp.where(keep[:, :, None], sigma_all, jnp.zeros((), jnp.bfloat16))
    piece = lax.all_gather(green, "row", axis=0, tiled=True)
    count = piece.shape[0]
    left = sigma_all.reshape(rows, count, orbit, orbit)
    right = piece.reshape(count, cols, orbit, orbit)
    history = jnp.einsum("asik,sbkj->abij", left, right, preferred_element_type=jnp.float32)
    collision = (step_size * history).astype(jnp.bfloat16).reshape(rows, cols, width)
    share = width // n_row
    finished = (
        green[rows - 1].astype(jnp.float32) + step_size * history[rows - 1].reshape(cols, width)
    ).astype(jnp.bfloat16)
    whole_row = from_root(finished, "row", n_row - 1)
    new_row = lax.dynamic_slice_in_dim(whole_row, lax.axis_index("row") * share, share, 1)
    return (collision, new_row)


def solution(mesh):
    placed = (P("row", "col", None), P())
    return jax.shard_map(
        shards,
        mesh=mesh,
        in_specs=placed,
        out_specs=(P("row", "col", None), P("col", "row")),
        check_vma=False,
    )
```

profile of v0, /device:TPU:2, one launch (start us, length us, event | category | flops | bytes accessed | tf_op | source)
XLA Modules:
  0.0 636.1 jit_solution(8872746443303099069)
XLA Ops:
  7.2 5.6 copy.15
  12.7 5.8 reshape.90
  18.5 19.5 %all_to_all.45 = bf16[16,2,4096]{2,1,0:T(2,128)(2,1)S(1)} all-to-all(bf16[16,2,4096]{2,1,0:T(2,128)(2,1)S(1)} %reshape.90), channel_id=1, replica_groups=mesh['row'=32,'col'=16] {'col'}, dimensions={0} | all-to-all | bytes 524288 | tf_op jit(solution)/shard_map/all_to_all | solution.py:19
  38.0 5.9 reshape.91
  43.9 6.0 copy.16
  49.9 26.2 %all_to_all.46 = bf16[4,128,256]{2,0,1:T(4,128)(2,1)S(1)} all-to-all(bf16[4,128,256]{2,0,1:T(4,128)(2,1)S(1)} %bitcast.48), channel_id=1, replica_groups=mesh['row'=32,'col'=16] {'row'}, dimensions={1} | all-to-all | bytes 524288 | tf_op jit(solution)/shard_map/all_to_all | solution.py:21
  76.2 0.8 copy.17
  77.0 4.8 all-to-all-start.2
  81.8 0.0 all-gather.3.cloned.1.call-start
  81.9 0.4 mul.61
  82.3 0.1 broadcast_multiply_fusion
  82.4 9.1 %all-to-all-done.2 = bf16[128,4,256]{2,1,0:T(4,128)(2,1)S(1)} async-done(((bf16[128,4,256]{2,1,0:T(4,128)(2,1)}), bf16[128,4,256]{2,1,0:T(4,128)(2,1)S(1)}, u32[]{:S(2)}, u32[]{:S(2)}) %all-to-all-start.2) | async-done | bytes 262176 | tf_op jit(solution)/shard_map/all_to_all | solution.py:20
  91.4 0.2 copy.34
  91.6 0.2 reshape.85
  91.8 0.3 copy.19
  92.1 0.2 fusion.5
  92.3 1.2 reshape.80
  93.5 0.0 all-gather.5.cloned.1.call-start
  93.6 0.7 all-gather.5.cloned.1.call-update
  94.3 0.0 all-reduce.2.cloned.1.call-start
  94.4 0.1 iota_compare_fusion
  94.4 76.5 %all-gather.3.cloned.1.call-done = bf16[4,128,4096]{2,1,0:T(8,128)(2,1)} async-done(((bf16[4,8,4096]{2,1,0:T(8,128)(2,1)}), bf16[4,128,4096]{2,1,0:T(8,128)(2,1)}) %all-gather.3.cloned.1.call-update) | async-done | bytes 4194320 | tf_op jit(solution)/shard_map/all_gather | solution.py:35
  170.9 4.5 broadcast_select_fusion
  175.4 6.3 copy.20
  181.7 157.9 %all-gather.5.cloned.1.call-done = bf16[128,8,4096]{2,1,0:T(8,128)(2,1)} async-done(((bf16[4,8,4096]{2,1,0:T(8,128)(2,1)}), bf16[128,8,4096]{2,1,0:T(8,128)(2,1)}) %all-gather.5.cloned.1.call-update) | async-done | bytes 8388624 | tf_op jit(solution)/shard_map/all_gather | solution.py:40
  339.7 12.5 %copy.21 = bf16[128,8,4096]{0,2,1:T(8,128)(2,1)} copy(bf16[128,8,4096]{2,1,0:T(8,128)(2,1)} %all-gather.5.cloned.1.call-done) | data formatting | bytes 16777216 | tf_op jit(solution)/shard_map/all_gather | solution.py:40
  352.2 7.9 %multiply_convert_fusion = (bf16[4,8,64,64]{3,2,1,0:T(8,128)(2,1)S(1)}, f32[4,8,64,64]{3,2,1,0:T(8,128)S(1)}) fusion(bf16[128,8,64,64,1]{0,3,2,1,4:T(8,128)(2,1)} %bitcast.44, bf16[4,128,64,64,1]{1,3,2,0,4:T(8,128)(2,1)} %bitcast.45), kind=kOutput, calls=%fused_computation.6 | convolution fusion | flops 2147745792 | bytes 13369344 | tf_op jit(solution)/shard_map/asik,sbkj->abij/dot_general | solution.py:44
  360.1 0.1 mul.68
  360.2 1.5 fusion.7
  361.7 1.2 reshape.83
  362.9 265.5 %all-reduce.2.cloned.1.call-done = bf16[8,4096]{1,0:T(8,128)(2,1)} async-done(((bf16[8,4096]{1,0:T(8,128)(2,1)}), bf16[8,4096]{1,0:T(8,128)(2,1)}) %all-reduce.2.cloned.1.call-update) | async-done | bytes 65552 | tf_op jit(solution)/shard_map/psum | solution.py:11
  628.3 1.2 constant_dynamic-slice_fusion
  (9 shorter events, 0.1 us)
Async XLA Ops:
  38.0 43.8 %copy-start = (bf16[4,8,4096]{2,1,0:T(8,128)(2,1)S(1)}, bf16[4,8,4096]{2,1,0:T(8,128)(2,1)}, u32[]{:S(2)}) copy-start(bf16[4,8,4096]{2,1,0:T(8,128)(2,1)} %param.2) | copy-start | bytes 786436
  43.9 38.4 %copy-start.1 = (f32[64]{0:T(128)S(1)}, f32[64]{0:T(128)}, u32[]{:S(2)}) copy-start(f32[64]{0:T(128)} %param.3) | copy-start | bytes 772
  77.0 14.5 %all-to-all-start.2 = ((bf16[128,4,256]{2,1,0:T(4,128)(2,1)}), bf16[128,4,256]{2,1,0:T(4,128)(2,1)S(1)}, u32[]{:S(2)}, u32[]{:S(2)}) async-start(bf16[128,4,256]{2,1,0:T(4,128)(2,1)} %bitcast.5), calls=%async_computation.2 | async-start | bytes 524288 | tf_op jit(solution)/shard_map/all_to_all | solution.py:20
  81.8 89.2 %all-gather.3.cloned.1.call-start = ((), (), s32[]{:S(2)}) async-start(), calls=%async_computation.3 | async-start | bytes 4456448 | tf_op jit(solution)/shard_map/all_gather | solution.py:35
  93.5 246.1 %all-gather.5.cloned.1.call-start = ((), (), s32[]{:S(2)}) async-start(), calls=%async_computation.4 | async-start | bytes 8650752 | tf_op jit(solution)/shard_map/all_gather | solution.py:40
  94.3 534.1 %all-reduce.2.cloned.1.call-start = ((), (), s32[]{:S(2)}) async-start(), calls=%async_computation.5 | async-start | bytes 131072 | tf_op jit(solution)/shard_map/psum | solution.py:11
Sparse Core Ops, SparseCore 0:
  93.7 77.2 all-gather.2
  173.0 166.6 all-gather.4
  361.8 266.4 all-reduce.1
where the time goes:
time: 637 us; the launch traced here: 636 us
  waiting for transfers between devices  510 us (80%)
  local copies, waits for them, and re-layouts  47.7 us (7%)
  blocking collectives  45.7 us (7%)
  between operations  13.8 us (2%)
  matrix products  7.89 us (1%)
    psum x1, waiting for transfers between devices, from_root(): return lax.psum(jnp.where(mine, x, jnp.zeros_like(x)), axis)  265 us
    all_gather x1, waiting for transfers between devices, shards(): piece = lax.all_gather(green, 'row', axis=0, tiled=True)  158 us
    all_gather x1, waiting for transfers between devices, shards(): sigma_all = lax.all_gather(sigma, 'col', axis=1, tiled=True)  76.5 us
    all_to_all x1, blocking collectives, shards(): lax.all_to_all(spread, 'row', split_axis=1, concat_axis=0, tiled=True)  26.2 us
    all_to_all x1, blocking collectives, shards(): lax.all_to_all(green, 'col', split_axis=2, concat_axis=1, tiled=True)  19.5 us
    unnamed x7, local copies, waits for them, and re-layouts  17.3 us
  transfers between devices with their start and end apart: 4, of which 4 were waited for; matrix products, arithmetic and copies ran while one was open for 2% of the time, Pallas kernels for 0%

commit v1 on v0

v1 whole, which is shorter than its diff:
```python
import jax
import jax.numpy as jnp
from jax import lax
from jax.experimental import pallas as pl
from jax.experimental.pallas import tpu as pltpu
from jax.sharding import PartitionSpec as P

step_size = 0.01
MESH = pl.DeviceIdType.MESH
BF = jnp.bfloat16
F32 = jnp.float32


def kernel(
    x_ref,
    pair_ref,
    out_ref,
    new_ref,
    gz,
    mir,
    own,
    sig,
    part,
    cin,
    acc,
    row_mid,
    row_src,
    row_in,
    g_send,
    g_recv,
    m_send,
    m_recv,
    s_send,
    s_recv,
    x_send,
    x_recv,
    k_send,
    k_recv,
    c_send,
    c_recv,
    n_send,
    n_recv,
):
    r = lax.axis_index("row")
    c = lax.axis_index("col")
    yl, z = r // 8, r % 8
    yh, x, k = c // 8, (c // 2) % 4, c % 2
    goal = c // 4
    half = (x // 2 + yl) % 2
    makes = yl >= goal

    def at(yl_, z_, yh_, x_, k_):
        return (yl_ * 8 + z_, yh_ * 8 + x_ * 2 + k_)

    def remote(src, dst, send, recv, device):
        return pltpu.make_async_remote_copy(
            src, dst, send, recv, device_id=device, device_id_type=MESH
        )

    up, down = at(yl, (z + 1) % 8, yh, x, k), at(yl, (z + 7) % 8, yh, x, k)
    other = at(yl, z, yh, x, 1 - k)

    def mirror_to(h):
        return (2 * c + h, r // 2)

    def mirror_from(b):
        return (2 * c + b, r // 2)

    itself = c == r // 2

    def stage_to(yh_, h):
        return at(goal, z, yh_, x if h == 0 else 3 - x, k)

    def stage_self(yh_, h):
        return (yl == goal) & (yh == yh_) if h == 0 else False

    def stage_from(y):
        return at(y, z, yl // 2, jnp.where(half == 0, x, 3 - x), k)

    def from_self(y):
        return (y == yl) & (yh == yl // 2) & (half == 0)

    barrier = pltpu.get_barrier_semaphore()

    def greet(device):
        pl.semaphore_signal(barrier, inc=1, device_id=device, device_id_type=MESH)

    greet(up)
    greet(down)
    greet(other)
    for d in (1, 2, 3):
        greet(at(yl, z, yh, (x + d) % 4, k))
    for b in range(2):

        @pl.when(makes & jnp.logical_not(itself & (z % 2 == b)))
        def _():
            greet(mirror_from(b))

    for y in range(4):

        @pl.when((y >= yl) & jnp.logical_not(from_self(y)))
        def _():
            greet(stage_from(y))

    for q in range(3):

        @pl.when(q < yl)
        def _():
            greet(at(q, z, yh, x, k))

    @pl.when(r != 31)
    def _():
        greet((31, c))

    peers = 9 - yl + jnp.where(r == 31, 31, 0)
    peers += jnp.where(goal >= yl, 2 - itself.astype(jnp.int32), 0)
    peers += jnp.where(makes, 4 - (yl == goal).astype(jnp.int32), 0)
    pl.semaphore_wait(barrier, peers)

    def mirror_copy(h):
        return remote(
            x_ref.at[:, pl.ds(h * 256, 256)],
            mir.at[z % 2],
            m_send.at[h],
            m_recv.at[z % 2],
            mirror_to(h),
        )

    def mirror_arrival(b):
        return remote(
            x_ref.at[:, pl.ds(0, 256)], mir.at[b], m_send.at[0], m_recv.at[b], up
        )

    for h in range(2):

        @pl.when((goal >= yl) & jnp.logical_not(itself & (z % 2 == h)))
        def _():
            mirror_copy(h).start()

        @pl.when(itself & (z % 2 == h))
        def _():
            mir[h] = x_ref[:, h * 256 : (h + 1) * 256]

    def g_copy(way, step):
        held = (z - step + 8) % 8 if way == 0 else (z + step) % 8
        rows = pl.ds(0, 256) if step < 3 else pl.ds(way * 128, 128)
        src = x_ref if step == 0 else gz.at[held]
        return remote(
            src.at[rows],
            gz.at[held, rows],
            g_send.at[way, step],
            g_recv.at[way, step],
            up if way == 0 else down,
        )

    def g_arrival(way, step):
        held = (z - step + 7) % 8 if way == 0 else (z + step + 1) % 8
        rows = pl.ds(0, 256) if step < 3 else pl.ds(way * 128, 128)
        return remote(
            x_ref.at[rows],
            gz.at[held, rows],
            g_send.at[way, step],
            g_recv.at[way, step],
            up,
        )

    def g_pass(step):
        for way in range(2):
            g_arrival(way, step - 1).wait_recv()
            g_copy(way, step).start()

    for way in range(2):
        g_copy(way, 0).start()
    gz[z] = x_ref[...]

    def stage_copy(yh_, h):
        return remote(
            own.at[pl.ds(h * 128, 128)],
            sig.at[yl, c % 4, pl.ds(h * 128, 128)],
            s_send.at[yh_ * 2 + h],
            s_recv.at[yl],
            stage_to(yh_, h),
        )

    def piece(x_, k_):
        h = (x_ // 2 + yl) % 2
        hi = (x_ + h) % 2
        return hi * 2 + k_, pl.ds(pl.multiple_of(h * 128, 128), 128)

    def stage_arrival(y):
        m, rows = piece(x, k)
        return remote(
            own.at[pl.ds(0, 128)], sig.at[y, m, rows], s_send.at[0], s_recv.at[y], up
        )

    @pl.when(makes)
    def _():
        for b in range(2):

            @pl.when(jnp.logical_not(itself & (z % 2 == b)))
            def _():
                mirror_arrival(b).wait_recv()

        for b in range(2):
            lanes = slice(b * 256, (b + 1) * 256)
            partner = mir[b].T
            later = lax.broadcasted_iota(jnp.int32, (64, 256), 1) // 64 + b * 4
            for i in range(4):
                rows = slice(i * 64, (i + 1) * 64)
                g = x_ref[rows, lanes].astype(F32)
                value = pair_ref[:, lanes] * (g * g) * partner[rows].astype(F32)
                keep = later <= 4 * r + i - 8 * c
                own[rows, lanes] = jnp.where(keep, value, 0.0).astype(BF)
        for yh_ in range(2):
            for h in range(2):
                if h == 1:
                    stage_copy(yh_, h).start()
                else:

                    @pl.when(jnp.logical_not(stage_self(yh_, h)))
                    def _():
                        stage_copy(yh_, h).start()

                    @pl.when(stage_self(yh_, h))
                    def _():
                        sig[yl, c % 4, 0:128] = own[0:128]

    def x_copy(y, d):
        m, rows = piece(x, k)
        return remote(
            sig.at[y, m, rows],
            sig.at[y, m, rows],
            x_send.at[y, d - 1],
            x_recv.at[y, d - 1],
            at(yl, z, yh, (x + d) % 4, k),
        )

    def x_arrival(y, d):
        m, rows = piece((x + 4 - d) % 4, k)
        return remote(
            own.at[pl.ds(0, 128)],
            sig.at[y, m, rows],
            x_send.at[y, d - 1],
            x_recv.at[y, d - 1],
            up,
        )

    def k_copy(y, d):
        m, rows = piece((x + 4 - d) % 4, k)
        return remote(
            sig.at[y, m, rows],
            sig.at[y, m, rows],
            k_send.at[y, d],
            k_recv.at[y, d],
            other,
        )

    def k_arrival(y, d):
        m, rows = piece((x + 4 - d) % 4, 1 - k)
        return remote(
            own.at[pl.ds(0, 128)],
            sig.at[y, m, rows],
            k_send.at[y, d],
            k_recv.at[y, d],
            other,
        )

    def spread(y):
        @pl.when(y >= yl)
        def _():
            @pl.when(jnp.logical_not(from_self(y)))
            def _():
                stage_arrival(y).wait_recv()

            for d in (2, 1, 3):
                x_copy(y, d).start()
            k_copy(y, 0).start()

    def swap(y):
        @pl.when(y >= yl)
        def _():
            for d in (1, 3, 2):
                x_arrival(y, d).wait_recv()
                k_copy(y, d).start()

    def c_copy(y):
        return remote(
            part.at[y - 1],
            cin.at[yl],
            c_send.at[y - 1],
            c_recv.at[yl],
            at(y, z, yh, x, k),
        )

    def c_arrival(q):
        return remote(part.at[0], cin.at[q], c_send.at[0], c_recv.at[q], up)

    def product(y):
        @pl.when(y >= yl)
        def _():
            for d in range(4):
                k_arrival(y, d).wait_recv()
            for m in range(4):
                term = jnp.dot(
                    sig[y, m],
                    gz[2 * m : 2 * m + 2].reshape(512, 512),
                    preferred_element_type=F32,
                )
                if m == 0:
                    acc[...] = term
                else:
                    acc[...] += term

        if y > 0:

            @pl.when(y > yl)
            def _():
                part[y - 1] = acc[...].astype(BF)
                c_copy(y).start()

    g_pass(1)
    spread(3)
    g_pass(2)
    spread(2)
    swap(3)
    g_pass(3)
    spread(1)
    swap(2)
    spread(0)
    for way in range(2):
        g_arrival(way, 3).wait_recv()
    product(3)
    swap(1)
    product(2)
    swap(0)
    product(1)
    product(0)

    for q in range(3):

        @pl.when(q < yl)
        def _():
            c_arrival(q).wait_recv()
            acc[...] += cin[q].astype(F32)

    out_ref[...] = (step_size * acc[...]).astype(BF)

    def n_copy(to):
        return remote(
            row_src.at[pl.ds(pl.multiple_of(to * 8, 8), 8)],
            row_in,
            n_send.at[to],
            n_recv,
            (to, c),
        )

    @pl.when(r == 31)
    def _():
        for q in range(4):
            lanes = slice(q * 128, (q + 1) * 128)
            row_mid[q * 64 : (q + 1) * 64, :] = (
                x_ref[192:256, lanes].astype(F32) + step_size * acc[192:256, lanes]
            )
            for i in range(2):
                row_src[pl.ds(i * 4 + q, 32, stride=8), :] = row_mid[
                    pl.ds(q * 64 + i, 32, stride=2), :
                ]

        @pl.loop(0, 31)
        def _(to):
            n_copy(to).start()

        row_in[...] = row_src[248:256, :]

        @pl.loop(0, 31)
        def _(to):
            n_copy(to).wait_send()

    @pl.when(r != 31)
    def _():
        n_copy(0).wait_recv()

    new_ref[...] = row_in[...]

    for h in range(2):

        @pl.when((goal >= yl) & jnp.logical_not(itself & (z % 2 == h)))
        def _():
            mirror_copy(h).wait_send()

    for step in range(4):
        for way in range(2):
            g_copy(way, step).wait_send()
    for yh_ in range(2):
        for h in range(2):

            @pl.when(makes & jnp.logical_not(stage_self(yh_, h)))
            def _():
                stage_copy(yh_, h).wait_send()

    for y in range(4):

        @pl.when(y >= yl)
        def _():
            for d in (1, 2, 3):
                x_copy(y, d).wait_send()
            for d in range(4):
                k_copy(y, d).wait_send()

        if y > 0:

            @pl.when(y > yl)
            def _():
                c_copy(y).wait_send()


def shards(green, coupling):
    rows, cols, width = green.shape
    orbit = coupling.shape[0]
    high, wide = rows * orbit, cols * orbit
    matrix = jnp.transpose(green.reshape(rows, cols, orbit, orbit), (0, 2, 1, 3))
    matrix = matrix.reshape(high, wide)
    pair = coupling[:, None] * jnp.tile(coupling, cols)[None, :]
    vmem = pl.BlockSpec(memory_space=pltpu.VMEM)
    dma = pltpu.SemaphoreType.DMA
    collision, fresh = pl.pallas_call(
        kernel,
        out_shape=(
            jax.ShapeDtypeStruct((high, wide), BF),
            jax.ShapeDtypeStruct((8, 128), F32),
        ),
        in_specs=[vmem, vmem],
        out_specs=(vmem, vmem),
        scratch_shapes=[
            pltpu.VMEM((8, high, wide), BF),
            pltpu.VMEM((2, high, high), BF),
            pltpu.VMEM((high, wide), BF),
            pltpu.VMEM((4, 4, high, wide), BF),
            pltpu.VMEM((3, high, wide), BF),
            pltpu.VMEM((3, high, wide), BF),
            pltpu.VMEM((high, wide), F32),
            pltpu.VMEM((256, 128), F32),
            pltpu.VMEM((256, 128), F32),
            pltpu.VMEM((8, 128), F32),
            dma((2, 4)),
            dma((2, 4)),
            dma((2,)),
            dma((2,)),
            dma((4,)),
            dma((4,)),
            dma((4, 3)),
            dma((4, 3)),
            dma((4, 4)),
            dma((4, 4)),
            dma((3,)),
            dma((3,)),
            dma((31,)),
            dma(()),
        ],
        compiler_params=pltpu.CompilerParams(
            collective_id=0, has_side_effects=True, vmem_limit_bytes=40 << 20
        ),
        cost_estimate=pl.CostEstimate(
            flops=2 * high * wide * 8192, bytes_accessed=4 * high * wide, transcendentals=0
        ),
        name="collide",
    )(matrix, pair)
    collision = collision.reshape(rows, orbit, cols, orbit).transpose(0, 2, 1, 3)
    collision = collision.reshape(rows, cols, width)
    fresh = fresh.reshape(2, 4, 2, orbit).transpose(1, 2, 0, 3).reshape(cols, 128)
    return (collision, fresh.astype(BF))


def solution(mesh):
    placed = (P("row", "col", None), P())
    return jax.shard_map(
        shards,
        mesh=mesh,
        in_specs=placed,
        out_specs=(P("row", "col", None), P("col", "row")),
        check_vma=False,
    )
```

time: 637 us -> 98.3 us (0.15)
  the two profiles are of different devices: /device:TPU:2 before, /device:TPU:46 now
where the time goes in v1:
time: 98.3 us; the launch traced here: 98.2 us
  Pallas kernels  92.6 us (94%)
  local copies, waits for them, and re-layouts  4.86 us (5%)
    pallas_call x1, Pallas kernels, shards(): pl.pallas_call(kernel, out_shape=(jax.ShapeDtypeStruct((high, wide), BF),...  92.6 us

profile of v1, /device:TPU:46, one launch (start us, length us, event | category | flops | bytes accessed | tf_op | source)
XLA Modules:
  0.0 98.2 jit_solution(9875149136184202921)
XLA Ops:
  0.6 1.5 %reshape.23 = bf16[4,8,64,64]{3,2,1,0:T(8,128)(2,1)S(1)} reshape(bf16[4,8,4096]{2,1,0:T(8,128)(2,1)} %param.2) | data formatting | bytes 524288 | tf_op jit(solution)/shard_map/reshape | solution.py:421
  2.1 0.3 copy.8
  2.5 0.0 copy-start
  2.5 0.3 reshape.24.x_ref
  2.8 0.3 copy-done
  3.1 0.1 mul.16
  3.2 0.1 broadcast_multiply_fusion.pair_ref
  3.3 92.6 %collide.1 = (bf16[256,512]{1,0:T(8,128)(2,1)S(1)}, f32[8,128]{1,0:T(8,128)S(1)}) custom-call(bf16[256,512]{1,0:T(8,128)(2,1)S(1)} %reshape.24.x_ref, f32[64,512]{1,0:T(8,128)S(1)} %broadcast_multiply_fusion.pair_ref), custom_call_target="tpu_custom_call" | custom-call | flops 2147483648 | bytes 524288 | tf_op jit(solution)/shard_map/collide/pallas_call | solution.py:426
  95.8 0.3 reshape.25
  96.1 0.1 copy.5
  96.2 1.2 %reshape.26 = bf16[4,8,4096]{2,1,0:T(8,128)(2,1)} reshape(bf16[4,8,64,64]{3,2,1,0:T(8,128)(2,1)S(1)} %copy.5) | data formatting | bytes 524288 | tf_op jit(solution)/shard_map/reshape | solution.py:469
  97.4 0.1 convert_element_type.13
  97.5 0.7 convert_element_type.15
  (3 shorter events, 0.0 us)
Async XLA Ops:
  2.5 0.7 copy-start

commit v2 on v1

v2 whole, which is shorter than its diff:
```python
import jax
import jax.numpy as jnp
from jax import lax
from jax.experimental import pallas as pl
from jax.experimental.pallas import tpu as pltpu
from jax.sharding import PartitionSpec as P

step_size = 0.01
MESH = pl.DeviceIdType.MESH
BF = jnp.bfloat16
F32 = jnp.float32


def kernel(
    x_ref,
    pair_ref,
    out_ref,
    new_ref,
    gz,
    mir,
    own,
    sig,
    part,
    cin,
    acc,
    row_mid,
    row_src,
    row_in,
    g_send,
    g_recv,
    m_send,
    m_recv,
    s_send,
    s_recv,
    y_send,
    y_recv,
    x_send,
    x_recv,
    k_send,
    k_recv,
    c_send,
    c_recv,
    f_send,
    f_recv,
    n_send,
    n_recv,
):
    r = lax.axis_index("row")
    c = lax.axis_index("col")
    yl, z = r // 8, r % 8
    yh, x, k = c // 8, (c // 2) % 4, c % 2
    goal = c // 4
    part_at = 2 * x + k

    def at(yl_, z_, yh_, x_, k_):
        return (yl_ * 8 + z_, yh_ * 8 + x_ * 2 + k_)

    def remote(src, dst, send, recv, device):
        return pltpu.make_async_remote_copy(
            src, dst, send, recv, device_id=device, device_id_type=MESH
        )

    up, down = at(yl, (z + 1) % 8, yh, x, k), at(yl, (z + 7) % 8, yh, x, k)
    other = at(yl, z, yh, x, 1 - k)
    across = at(yl, z, 1 - yh, x, k)

    gives_mirror = goal >= yl

    def mirror_to(h):
        return at(yl, (x % 2) * 4 + k * 2 + h, yh, z // 2, z % 2)

    def mirror_self(h):
        return (z == part_at) & (z == (x % 2) * 4 + k * 2 + h)

    def mirror_from(s):
        return at(yl, part_at, yh, s * 2 + z // 4, (z // 2) % 2)

    def mirror_from_self(s):
        return (z == part_at) & (x == s * 2 + z // 4) & (k == (z // 2) % 2)

    gives_piece = yl >= goal

    def piece_to(h):
        return at(goal, z, yl // 2, (x % 2) * 2 + k, h)

    def piece_self(h):
        return (goal == yl) & (x == (x % 2) * 2 + k) & (k == h)

    def piece_from(s):
        return at(2 * yh + s, z, yl // 2, (yl % 2) * 2 + x // 2, x % 2)

    def piece_from_self(s):
        mine = (2 * yh + s == yl) & (x == (yl % 2) * 2 + x // 2) & (k == x % 2)
        return mine & (yl // 2 == yh)

    def one(flag):
        return jnp.where(flag, 1, 0)

    barrier = pltpu.get_barrier_semaphore()

    def greet(device):
        pl.semaphore_signal(barrier, inc=1, device_id=device, device_id_type=MESH)

    greet(up)
    greet(down)
    greet(other)
    for d in (1, 2, 3):
        greet(at(yl, z, yh, (x + d) % 4, k))
    for s in range(2):

        @pl.when((2 * yh + s >= yl) & jnp.logical_not(mirror_from_self(s)))
        def _():
            greet(mirror_from(s))

        @pl.when((2 * yh + s >= yl) & jnp.logical_not(piece_from_self(s)))
        def _():
            greet(piece_from(s))

    @pl.when(3 - 2 * yh >= yl)
    def _():
        greet(across)

    for q in range(3):

        @pl.when(q < yl)
        def _():
            greet(at(q, z, yh, x, k))

    @pl.when(z != 7)
    def _():
        greet(at(yl, 7, yh, x, k))

    @pl.when((z == 7) & (yl != 3))
    def _():
        greet((31, c))

    peers = 9 - yl + jnp.where(z == 7, 7, 0) + jnp.where(r == 31, 3, 0)
    peers += one(2 * yh + 1 >= yl)
    for h in range(2):
        peers += one(gives_mirror & jnp.logical_not(mirror_self(h)))
        peers += one(gives_piece & jnp.logical_not(piece_self(h)))
    pl.semaphore_wait(barrier, peers)

    def half_of(h):
        return x_ref.at[:, pl.ds(h * 256, 256)]

    def mirror_copy(h):
        return remote(
            half_of(h), mir.at[x // 2], m_send.at[h], m_recv.at[x // 2], mirror_to(h)
        )

    def mirror_arrival(s):
        return remote(half_of(0), mir.at[s], m_send.at[0], m_recv.at[s], up)

    def piece_copy(h):
        return remote(
            half_of(h), own.at[yl % 2], s_send.at[h], s_recv.at[yl % 2], piece_to(h)
        )

    def piece_arrival(s):
        return remote(half_of(0), own.at[s], s_send.at[0], s_recv.at[s], up)

    for h in range(2):

        @pl.when(gives_mirror & jnp.logical_not(mirror_self(h)))
        def _():
            mirror_copy(h).start()

        @pl.when(gives_piece & jnp.logical_not(piece_self(h)))
        def _():
            piece_copy(h).start()

        @pl.when(gives_mirror & mirror_self(h))
        def _():
            mir[x // 2] = x_ref[:, h * 256 : (h + 1) * 256]

        @pl.when(gives_piece & piece_self(h))
        def _():
            own[yl % 2] = x_ref[:, h * 256 : (h + 1) * 256]

    def g_copy(way, step):
        held = (z - step + 8) % 8 if way == 0 else (z + step) % 8
        rows = pl.ds(0, 256) if step < 3 else pl.ds(way * 128, 128)
        src = x_ref if step == 0 else gz.at[held]
        return remote(
            src.at[rows],
            gz.at[held, rows],
            g_send.at[way, step],
            g_recv.at[way, step],
            up if way == 0 else down,
        )

    def g_arrival(way, step):
        held = (z - step + 7) % 8 if way == 0 else (z + step + 1) % 8
        rows = pl.ds(0, 256) if step < 3 else pl.ds(way * 128, 128)
        return remote(
            x_ref.at[rows],
            gz.at[held, rows],
            g_send.at[way, step],
            g_recv.at[way, step],
            up,
        )

    def g_pass(step):
        for way in range(2):
            g_arrival(way, step - 1).wait_recv()
            g_copy(way, step).start()

    for way in range(2):
        g_copy(way, 0).start()
    gz[z] = x_ref[...]

    def y_copy(y):
        return remote(
            sig.at[y, part_at], sig.at[y, part_at], y_send.at[y], y_recv.at[y], across
        )

    def x_copy(y, d):
        return remote(
            sig.at[y, part_at],
            sig.at[y, part_at],
            x_send.at[y, d - 1],
            x_recv.at[y, d - 1],
            at(yl, z, yh, (x + d) % 4, k),
        )

    def x_arrival(y, d):
        j = 2 * ((x + 4 - d) % 4) + k
        return remote(
            sig.at[y, j], sig.at[y, j], x_send.at[y, d - 1], x_recv.at[y, d - 1], up
        )

    def k_copy(y, d):
        j = 2 * ((x + 4 - d) % 4) + k
        return remote(
            sig.at[y, j], sig.at[y, j], k_send.at[y, d], k_recv.at[y, d], other
        )

    def k_arrival(y, d):
        j = 2 * ((x + 4 - d) % 4) + 1 - k
        return remote(
            sig.at[y, j], sig.at[y, j], k_send.at[y, d], k_recv.at[y, d], other
        )

    def spread(y):
        for d in (1, 3, 2):
            x_copy(y, d).start()
        k_copy(y, 0).start()

    def near(i):
        return 2 * yh + 1 - i

    def far(i):
        return 3 - 2 * yh - i

    def make(i):
        s = 1 - i
        y = near(i)

        @pl.when(y >= yl)
        def _():
            @pl.when(jnp.logical_not(mirror_from_self(s)))
            def _():
                mirror_arrival(s).wait_recv()

            @pl.when(jnp.logical_not(piece_from_self(s)))
            def _():
                piece_arrival(s).wait_recv()

            partner = mir[s].T
            pair = pair_ref[:, 0:256]
            later = lax.broadcasted_iota(jnp.int32, (64, 256), 1) // 64
            first = 32 * (y - yl) + 4 * z - 4 * part_at
            for i in range(4):
                rows = slice(i * 64, (i + 1) * 64)
                g = own[s, rows, :].astype(F32)
                value = pair * (g * g) * partner[rows].astype(F32)
                keep = later <= first + i
                sig[y, part_at, rows, :] = jnp.where(keep, value, 0.0).astype(BF)
            y_copy(y).start()
            spread(y)

    def hand_on(i):
        y = far(i)

        @pl.when(y >= yl)
        def _():
            y_copy(y).wait_recv()
            spread(y)

    def swap(y):
        @pl.when(y >= yl)
        def _():
            for d in (1, 3, 2):
                x_arrival(y, d).wait_recv()
                k_copy(y, d).start()

    def c_copy(y):
        return remote(
            part.at[y - 1],
            cin.at[yl],
            c_send.at[y - 1],
            c_recv.at[yl],
            at(y, z, yh, x, k),
        )

    def c_arrival(q):
        return remote(part.at[0], cin.at[q], c_send.at[0], c_recv.at[q], up)

    def product(y):
        @pl.when(y >= yl)
        def _():
            for d in range(4):
                k_arrival(y, d).wait_recv()
            total = jnp.zeros((256, 512), F32)
            for j in range(8):
                total += jnp.dot(sig[y, j], gz[j], preferred_element_type=F32)

            @pl.when(y > yl)
            def _():
                part[y - 1] = total.astype(BF)
                c_copy(y).start()

            @pl.when(y == yl)
            def _():
                acc[...] = total

    g_pass(1)
    make(0)
    make(1)
    g_pass(2)
    swap(near(0))
    swap(near(1))
    hand_on(0)
    g_pass(3)
    hand_on(1)
    for way in range(2):
        g_arrival(way, 3).wait_recv()
    product(near(0))
    product(near(1))
    swap(far(0))
    product(far(0))
    swap(far(1))
    product(far(1))

    for q in range(3):

        @pl.when(q < yl)
        def _():
            c_arrival(q).wait_recv()
            acc[...] += cin[q].astype(F32)

    out_ref[...] = (step_size * acc[...]).astype(BF)

    def far_copy(y):
        return remote(
            row_src.at[pl.ds(y * 64, 64)],
            row_src.at[pl.ds(y * 64, 64)],
            f_send.at[y],
            f_recv,
            at(y, 7, yh, x, k),
        )

    def n_copy(to):
        return remote(
            row_src.at[pl.ds(pl.multiple_of(yl * 64 + to * 8, 8), 8)],
            row_in,
            n_send.at[to],
            n_recv,
            at(yl, to, yh, x, k),
        )

    @pl.when(r == 31)
    def _():
        for q in range(4):
            lanes = slice(q * 128, (q + 1) * 128)
            row_mid[q * 64 : (q + 1) * 64, :] = (
                x_ref[192:256, lanes].astype(F32) + step_size * acc[192:256, lanes]
            )
            for i in range(2):
                row_src[pl.ds(i * 4 + q, 32, stride=8), :] = row_mid[
                    pl.ds(q * 64 + i, 32, stride=2), :
                ]
        for y in range(3):
            far_copy(y).start()

    @pl.when(z == 7)
    def _():
        @pl.when(yl != 3)
        def _():
            remote(
                row_src.at[pl.ds(0, 64)],
                row_src.at[pl.ds(pl.multiple_of(yl * 64, 64), 64)],
                f_send.at[0],
                f_recv,
                other,
            ).wait_recv()

        for to in range(7):
            n_copy(to).start()
        row_in[...] = row_src[pl.ds(pl.multiple_of(yl * 64 + 56, 8), 8), :]
        for to in range(7):
            n_copy(to).wait_send()

    @pl.when(z != 7)
    def _():
        n_copy(0).wait_recv()

    @pl.when(r == 31)
    def _():
        for y in range(3):
            far_copy(y).wait_send()

    new_ref[...] = row_in[...]

    for h in range(2):

        @pl.when(gives_mirror & jnp.logical_not(mirror_self(h)))
        def _():
            mirror_copy(h).wait_send()

        @pl.when(gives_piece & jnp.logical_not(piece_self(h)))
        def _():
            piece_copy(h).wait_send()

    for step in range(4):
        for way in range(2):
            g_copy(way, step).wait_send()
    for i in range(2):

        @pl.when(near(i) >= yl)
        def _():
            y_copy(near(i)).wait_send()

    for y in range(4):

        @pl.when(y >= yl)
        def _():
            for d in (1, 2, 3):
                x_copy(y, d).wait_send()
            for d in range(4):
                k_copy(y, d).wait_send()

        if y > 0:

            @pl.when(y > yl)
            def _():
                c_copy(y).wait_send()


def shards(green, coupling):
    rows, cols, width = green.shape
    orbit = coupling.shape[0]
    high, wide = rows * orbit, cols * orbit
    matrix = jnp.transpose(green.reshape(rows, cols, orbit, orbit), (0, 2, 1, 3))
    matrix = matrix.reshape(high, wide)
    pair = coupling[:, None] * jnp.tile(coupling, cols)[None, :]
    vmem = pl.BlockSpec(memory_space=pltpu.VMEM)
    dma = pltpu.SemaphoreType.DMA
    collision, fresh = pl.pallas_call(
        kernel,
        out_shape=(
            jax.ShapeDtypeStruct((high, wide), BF),
            jax.ShapeDtypeStruct((8, 128), F32),
        ),
        in_specs=[vmem, vmem],
        out_specs=(vmem, vmem),
        scratch_shapes=[
            pltpu.VMEM((8, high, wide), BF),
            pltpu.VMEM((2, high, high), BF),
            pltpu.VMEM((2, high, high), BF),
            pltpu.VMEM((4, 8, high, high), BF),
            pltpu.VMEM((3, high, wide), BF),
            pltpu.VMEM((3, high, wide), BF),
            pltpu.VMEM((high, wide), F32),
            pltpu.VMEM((256, 128), F32),
            pltpu.VMEM((256, 128), F32),
            pltpu.VMEM((8, 128), F32),
            dma((2, 4)),
            dma((2, 4)),
            dma((2,)),
            dma((2,)),
            dma((2,)),
            dma((2,)),
            dma((4,)),
            dma((4,)),
            dma((4, 3)),
            dma((4, 3)),
            dma((4, 4)),
            dma((4, 4)),
            dma((3,)),
            dma((3,)),
            dma((3,)),
            dma(()),
            dma((7,)),
            dma(()),
        ],
        compiler_params=pltpu.CompilerParams(
            collective_id=0, has_side_effects=True, vmem_limit_bytes=40 << 20
        ),
        cost_estimate=pl.CostEstimate(
            flops=2 * high * wide * 8192, bytes_accessed=4 * high * wide, transcendentals=0
        ),
        name="collide",
    )(matrix, pair)
    collision = collision.reshape(rows, orbit, cols, orbit).transpose(0, 2, 1, 3)
    collision = collision.reshape(rows, cols, width)
    fresh = fresh.reshape(2, 4, 2, orbit).transpose(1, 2, 0, 3).reshape(cols, 128)
    return (collision, fresh.astype(BF))


def solution(mesh):
    placed = (P("row", "col", None), P())
    return jax.shard_map(
        shards,
        mesh=mesh,
        in_specs=placed,
        out_specs=(P("row", "col", None), P("col", "row")),
        check_vma=False,
    )
```

time: 98.3 us -> 85 us (0.86)
  the two profiles are of different devices: /device:TPU:46 before, /device:TPU:21 now
where the time goes in v2:
time: 85 us; the launch traced here: 84.8 us
  Pallas kernels  79.2 us (93%)
  local copies, waits for them, and re-layouts  4.86 us (6%)
    pallas_call x1, Pallas kernels, shards(): pl.pallas_call(kernel, out_shape=(jax.ShapeDtypeStruct((high, wide), BF),...  79.2 us
    reshape x2, local copies, waits for them, and re-layouts, shards(): green.reshape(rows, cols, orbit, orbit)  1.82 us

profile of v2, /device:TPU:21, one launch (start us, length us, event | category | flops | bytes accessed | tf_op | source)
XLA Modules:
  0.0 84.8 jit_solution(4237583685007442993)
XLA Ops:
  0.6 1.5 %reshape.23 = bf16[4,8,64,64]{3,2,1,0:T(8,128)(2,1)S(1)} reshape(bf16[4,8,4096]{2,1,0:T(8,128)(2,1)} %param.2) | data formatting | bytes 524288 | tf_op jit(solution)/shard_map/reshape | solution.py:455
  2.1 0.3 copy.8
  2.5 0.0 copy-start
  2.5 0.3 reshape.24.x_ref
  2.8 0.3 copy-done
  3.1 0.1 mul.16
  3.2 0.1 broadcast_multiply_fusion.pair_ref
  3.3 79.2 %collide.1 = (bf16[256,512]{1,0:T(8,128)(2,1)S(1)}, f32[8,128]{1,0:T(8,128)S(1)}) custom-call(bf16[256,512]{1,0:T(8,128)(2,1)S(1)} %reshape.24.x_ref, f32[64,512]{1,0:T(8,128)S(1)} %broadcast_multiply_fusion.pair_ref), custom_call_target="tpu_custom_call" | custom-call | flops 2147483648 | bytes 524288 | tf_op jit(solution)/shard_map/collide/pallas_call | solution.py:460
  82.5 0.3 reshape.25
  82.8 0.1 copy.5
  82.9 1.2 %reshape.26 = bf16[4,8,4096]{2,1,0:T(8,128)(2,1)} reshape(bf16[4,8,64,64]{3,2,1,0:T(8,128)(2,1)S(1)} %copy.5) | data formatting | bytes 524288 | tf_op jit(solution)/shard_map/reshape | solution.py:507
  84.1 0.1 convert_element_type.13
  84.2 0.7 convert_element_type.15
  (3 shorter events, 0.0 us)
Async XLA Ops:
  2.5 0.7 copy-start

commit v3 on v2

--- a/solution.py
+++ b/solution.py
@@ -64,19 +64,13 @@
     other = at(yl, z, yh, x, 1 - k)
     across = at(yl, z, 1 - yh, x, k)
 
-    gives_mirror = goal >= yl
-
-    def mirror_to(h):
-        return at(yl, (x % 2) * 4 + k * 2 + h, yh, z // 2, z % 2)
-
-    def mirror_self(h):
-        return (z == part_at) & (z == (x % 2) * 4 + k * 2 + h)
+    lends = (z // 2 == (x % 2) * 2 + k) & (goal >= yl)
 
     def mirror_from(s):
-        return at(yl, part_at, yh, s * 2 + z // 4, (z // 2) % 2)
+        return at(yl, z, yh, s * 2 + z // 4, (z // 2) % 2)
 
     def mirror_from_self(s):
-        return (z == part_at) & (x == s * 2 + z // 4) & (k == (z // 2) % 2)
+        return (x == s * 2 + z // 4) & (k == (z // 2) % 2)
 
     gives_piece = yl >= goal
 
@@ -135,80 +129,89 @@
         greet((31, c))
 
     peers = 9 - yl + jnp.where(z == 7, 7, 0) + jnp.where(r == 31, 3, 0)
-    peers += one(2 * yh + 1 >= yl)
+    peers += one(2 * yh + 1 >= yl) + jnp.where(lends, 7, 0)
     for h in range(2):
-        peers += one(gives_mirror & jnp.logical_not(mirror_self(h)))
         peers += one(gives_piece & jnp.logical_not(piece_self(h)))
     pl.semaphore_wait(barrier, peers)
 
     def half_of(h):
         return x_ref.at[:, pl.ds(h * 256, 256)]
 
-    def mirror_copy(h):
-        return remote(
-            half_of(h), mir.at[x // 2], m_send.at[h], m_recv.at[x // 2], mirror_to(h)
+    def piece_copy(h):
+        return remote(
+            half_of(h), own.at[yl % 2], s_send.at[h], s_recv.at[yl % 2], piece_to(h)
+        )
+
+    def piece_arrival(s):
+        return remote(half_of(0), own.at[s], s_send.at[0], s_recv.at[s], up)
+
+    def g_copy(way, step, rows):
+        held = (z - step + 8) % 8 if way == 0 else (z + step) % 8
+        src = x_ref if step == 0 else gz.at[held]
+        return remote(
+            src.at[pl.ds(rows * 128, 128)],
+            gz.at[held, pl.ds(rows * 128, 128)],
+            g_send.at[way, step, rows],
+            g_recv.at[way, step, rows],
+            up if way == 0 else down,
+        )
+
+    def g_arrival(way, step, rows):
+        held = (z - step + 7) % 8 if way == 0 else (z + step + 1) % 8
+        return remote(
+            x_ref.at[pl.ds(0, 128)],
+            gz.at[held, pl.ds(rows * 128, 128)],
+            g_send.at[way, step, rows],
+            g_recv.at[way, step, rows],
+            up,
+        )
+
+    def g_pass(step):
+        for rows in range(2):
+            for way in range(2):
+                g_arrival(way, step - 1, rows).wait_recv()
+                if step < 3 or rows == way:
+                    g_copy(way, step, rows).start()
+
+    def mirror_copy(b):
+        lanes = pl.ds(pl.multiple_of((z % 2) * 256, 256), 256)
+        return remote(
+            gz.at[b, :, lanes],
+            mir.at[x // 2],
+            m_send.at[b],
+            m_recv.at[x // 2],
+            at(yl, z, yh, b // 2, b % 2),
         )
 
     def mirror_arrival(s):
         return remote(half_of(0), mir.at[s], m_send.at[0], m_recv.at[s], up)
 
-    def piece_copy(h):
-        return remote(
-            half_of(h), own.at[yl % 2], s_send.at[h], s_recv.at[yl % 2], piece_to(h)
-        )
-
-    def piece_arrival(s):
-        return remote(half_of(0), own.at[s], s_send.at[0], s_recv.at[s], up)
-
+    def lend(b):
+        @pl.when(lends & (b != part_at))
+        def _():
+            mirror_copy(b).start()
+
+        for h in range(2):
+
+            @pl.when(lends & (b == part_at) & (z % 2 == h))
+            def _():
+                mir[x // 2] = gz[b, :, h * 256 : (h + 1) * 256]
+
+    for rows in range(2):
+        for way in range(2):
+            g_copy(way, 0, rows).start()
     for h in range(2):
 
-        @pl.when(gives_mirror & jnp.logical_not(mirror_self(h)))
-        def _():
-            mirror_copy(h).start()
-
         @pl.when(gives_piece & jnp.logical_not(piece_self(h)))
         def _():
             piece_copy(h).start()
 
-        @pl.when(gives_mirror & mirror_self(h))
-        def _():
-            mir[x // 2] = x_ref[:, h * 256 : (h + 1) * 256]
-
         @pl.when(gives_piece & piece_self(h))
         def _():
             own[yl % 2] = x_ref[:, h * 256 : (h + 1) * 256]
 
-    def g_copy(way, step):
-        held = (z - step + 8) % 8 if way == 0 else (z + step) % 8
-        rows = pl.ds(0, 256) if step < 3 else pl.ds(way * 128, 128)
-        src = x_ref if step == 0 else gz.at[held]
-        return remote(
-            src.at[rows],
-            gz.at[held, rows],
-            g_send.at[way, step],
-            g_recv.at[way, step],
-            up if way == 0 else down,
-        )
-
-    def g_arrival(way, step):
-        held = (z - step + 7) % 8 if way == 0 else (z + step + 1) % 8
-        rows = pl.ds(0, 256) if step < 3 else pl.ds(way * 128, 128)
-        return remote(
-            x_ref.at[rows],
-            gz.at[held, rows],
-            g_send.at[way, step],
-            g_recv.at[way, step],
-            up,
-        )
-
-    def g_pass(step):
-        for way in range(2):
-            g_arrival(way, step - 1).wait_recv()
-            g_copy(way, step).start()
-
-    for way in range(2):
-        g_copy(way, 0).start()
     gz[z] = x_ref[...]
+    lend(z)
 
     def y_copy(y):
         return remote(
@@ -325,17 +328,38 @@
             def _():
                 acc[...] = total
 
-    g_pass(1)
-    make(0)
-    make(1)
-    g_pass(2)
+    gap = (part_at - z + 8) % 8
+    gap = jnp.minimum(gap, 8 - gap)
+
+    for step in range(1, 5):
+        if step < 4:
+            g_pass(step)
+            lend((z - step + 8) % 8)
+            lend((z + step) % 8)
+        else:
+            for way in range(2):
+                g_arrival(way, 3, way).wait_recv()
+            lend((z + 4) % 8)
+        if step > 1:
+
+            @pl.when(jnp.maximum(gap, 1) == step - 1)
+            def _():
+                hand_on(0)
+                hand_on(1)
+
+        @pl.when(jnp.maximum(gap, 1) == step)
+        def _():
+            make(0)
+            make(1)
+
     swap(near(0))
     swap(near(1))
-    hand_on(0)
-    g_pass(3)
-    hand_on(1)
-    for way in range(2):
-        g_arrival(way, 3).wait_recv()
+
+    @pl.when(gap == 4)
+    def _():
+        hand_on(0)
+        hand_on(1)
+
     product(near(0))
     product(near(1))
     swap(far(0))
@@ -415,17 +439,21 @@
 
     for h in range(2):
 
-        @pl.when(gives_mirror & jnp.logical_not(mirror_self(h)))
-        def _():
-            mirror_copy(h).wait_send()
-
         @pl.when(gives_piece & jnp.logical_not(piece_self(h)))
         def _():
             piece_copy(h).wait_send()
+
+    for b in range(8):
+
+        @pl.when(lends & (b != part_at))
+        def _():
+            mirror_copy(b).wait_send()
 
     for step in range(4):
         for way in range(2):
-            g_copy(way, step).wait_send()
+            for rows in range(2):
+                if step < 3 or rows == way:
+                    g_copy(way, step, rows).wait_send()
     for i in range(2):
 
         @pl.when(near(i) >= yl)
@@ -476,9 +504,9 @@
             pltpu.VMEM((256, 128), F32),
             pltpu.VMEM((256, 128), F32),
             pltpu.VMEM((8, 128), F32),
-            dma((2, 4)),
-            dma((2, 4)),
-            dma((2,)),
+            dma((2, 4, 2)),
+            dma((2, 4, 2)),
+            dma((8,)),
             dma((2,)),
             dma((2,)),
             dma((2,)),

time: 85 us -> 101 us (1.19)
  the two profiles are of different devices: /device:TPU:21 before, /device:TPU:22 now
where the time goes in v3:
time: 101 us
  Pallas kernels  95.1 us (94%)
  local copies, waits for them, and re-layouts  4.86 us (5%)
    pallas_call x1, Pallas kernels, shards(): pl.pallas_call(kernel, out_shape=(jax.ShapeDtypeStruct((high, wide), BF),...  95.1 us

profile of v3, /device:TPU:22, one launch (start us, length us, event | category | flops | bytes accessed | tf_op | source)
XLA Modules:
  0.0 100.7 jit_solution(7494285872668605782)
XLA Ops:
  0.6 1.5 %reshape.23 = bf16[4,8,64,64]{3,2,1,0:T(8,128)(2,1)S(1)} reshape(bf16[4,8,4096]{2,1,0:T(8,128)(2,1)} %param.2) | data formatting | bytes 524288 | tf_op jit(solution)/shard_map/reshape | solution.py:483
  2.1 0.3 copy.8
  2.5 0.0 copy-start
  2.5 0.3 reshape.24.x_ref
  2.8 0.3 copy-done
  3.1 0.1 mul.16
  3.2 0.1 broadcast_multiply_fusion.pair_ref
  3.3 95.1 %collide.1 = (bf16[256,512]{1,0:T(8,128)(2,1)S(1)}, f32[8,128]{1,0:T(8,128)S(1)}) custom-call(bf16[256,512]{1,0:T(8,128)(2,1)S(1)} %reshape.24.x_ref, f32[64,512]{1,0:T(8,128)S(1)} %broadcast_multiply_fusion.pair_ref), custom_call_target="tpu_custom_call" | custom-call | flops 2147483648 | bytes 524288 | tf_op jit(solution)/shard_map/collide/pallas_call | solution.py:488
  98.3 0.3 reshape.25
  98.6 0.1 copy.5
  98.7 1.2 %reshape.26 = bf16[4,8,4096]{2,1,0:T(8,128)(2,1)} reshape(bf16[4,8,64,64]{3,2,1,0:T(8,128)(2,1)S(1)} %copy.5) | data formatting | bytes 524288 | tf_op jit(solution)/shard_map/reshape | solution.py:535
  99.9 0.1 convert_element_type.13
  100.0 0.7 convert_element_type.15
  (3 shorter events, 0.0 us)
Async XLA Ops:
  2.5 0.7 copy-start

commit v4 on v3

--- a/solution.py
+++ b/solution.py
@@ -23,6 +23,7 @@
     part,
     cin,
     acc,
+    held,
     row_mid,
     row_src,
     row_in,
@@ -36,6 +37,8 @@
     y_recv,
     x_send,
     x_recv,
+    h_send,
+    h_recv,
     k_send,
     k_recv,
     c_send,
@@ -50,7 +53,17 @@
     yl, z = r // 8, r % 8
     yh, x, k = c // 8, (c // 2) % 4, c % 2
     goal = c // 4
-    part_at = 2 * x + k
+
+    def part_of(x_):
+        m = jnp.where((x_ == 1) | (x_ == 2), 2, 0) + x_ // 2
+        return 2 * jnp.where(yl % 2 == 0, m, 3 - m) + k
+
+    def place_of(j):
+        m = jnp.where(yl % 2 == 0, j // 2, 3 - j // 2)
+        return jnp.where(m == 1, 3, (m + 1) // 2)
+
+    part_at = part_of(x)
+    m_at = part_at // 2
 
     def at(yl_, z_, yh_, x_, k_):
         return (yl_ * 8 + z_, yh_ * 8 + x_ * 2 + k_)
@@ -64,28 +77,37 @@
     other = at(yl, z, yh, x, 1 - k)
     across = at(yl, z, 1 - yh, x, k)
 
-    lends = (z // 2 == (x % 2) * 2 + k) & (goal >= yl)
+    gives_mirror = goal >= yl
+
+    def mirror_to(h):
+        return at(yl, (x % 2) * 4 + k * 2 + h, yh, place_of(z), z % 2)
+
+    def mirror_self(h):
+        return (z == part_at) & (z == (x % 2) * 4 + k * 2 + h)
 
     def mirror_from(s):
-        return at(yl, z, yh, s * 2 + z // 4, (z // 2) % 2)
+        return at(yl, part_at, yh, s * 2 + z // 4, (z // 2) % 2)
 
     def mirror_from_self(s):
-        return (x == s * 2 + z // 4) & (k == (z // 2) % 2)
+        return (z == part_at) & (x == s * 2 + z // 4) & (k == (z // 2) % 2)
 
     gives_piece = yl >= goal
 
     def piece_to(h):
-        return at(goal, z, yl // 2, (x % 2) * 2 + k, h)
+        return at(goal, z, yl // 2, (x + 4 + k * (2 * (x % 2) - 1)) % 4, h)
 
     def piece_self(h):
-        return (goal == yl) & (x == (x % 2) * 2 + k) & (k == h)
+        return (goal == yl) & (k == 0) if h == 0 else False
 
     def piece_from(s):
-        return at(2 * yh + s, z, yl // 2, (yl % 2) * 2 + x // 2, x % 2)
+        return at(2 * yh + s, z, yl // 2, (yl % 2) * 2 + m_at // 2, m_at % 2)
 
     def piece_from_self(s):
-        mine = (2 * yh + s == yl) & (x == (yl % 2) * 2 + x // 2) & (k == x % 2)
+        mine = (2 * yh + s == yl) & (x == (yl % 2) * 2 + m_at // 2) & (k == m_at % 2)
         return mine & (yl // 2 == yh)
+
+    def adds(q):
+        return (q < yl) & ((yl != 2) | (q == 1))
 
     def one(flag):
         return jnp.where(flag, 1, 0)
@@ -98,7 +120,7 @@
     greet(up)
     greet(down)
     greet(other)
-    for d in (1, 2, 3):
+    for d in (1, 3):
         greet(at(yl, z, yh, (x + d) % 4, k))
     for s in range(2):
 
@@ -116,7 +138,7 @@
 
     for q in range(3):
 
-        @pl.when(q < yl)
+        @pl.when(adds(q))
         def _():
             greet(at(q, z, yh, x, k))
 
@@ -128,9 +150,10 @@
     def _():
         greet((31, c))
 
-    peers = 9 - yl + jnp.where(z == 7, 7, 0) + jnp.where(r == 31, 3, 0)
-    peers += one(2 * yh + 1 >= yl) + jnp.where(lends, 7, 0)
+    peers = 5 + jnp.minimum(3 - yl, 2) + jnp.where(z == 7, 7, 0) + jnp.where(r == 31, 3, 0)
+    peers += one(2 * yh + 1 >= yl)
     for h in range(2):
+        peers += one(gives_mirror & jnp.logical_not(mirror_self(h)))
         peers += one(gives_piece & jnp.logical_not(piece_self(h)))
     pl.semaphore_wait(barrier, peers)
 
@@ -173,29 +196,23 @@
                 if step < 3 or rows == way:
                     g_copy(way, step, rows).start()
 
-    def mirror_copy(b):
-        lanes = pl.ds(pl.multiple_of((z % 2) * 256, 256), 256)
-        return remote(
-            gz.at[b, :, lanes],
-            mir.at[x // 2],
-            m_send.at[b],
-            m_recv.at[x // 2],
-            at(yl, z, yh, b // 2, b % 2),
+    def mirror_copy(h):
+        return remote(
+            half_of(h), mir.at[x // 2], m_send.at[h], m_recv.at[x // 2], mirror_to(h)
         )
 
     def mirror_arrival(s):
         return remote(half_of(0), mir.at[s], m_send.at[0], m_recv.at[s], up)
 
-    def lend(b):
-        @pl.when(lends & (b != part_at))
-        def _():
-            mirror_copy(b).start()
-
-        for h in range(2):
-
-            @pl.when(lends & (b == part_at) & (z % 2 == h))
-            def _():
-                mir[x // 2] = gz[b, :, h * 256 : (h + 1) * 256]
+    for h in range(2):
+
+        @pl.when(gives_mirror & jnp.logical_not(mirror_self(h)))
+        def _():
+            mirror_copy(h).start()
+
+        @pl.when(gives_mirror & mirror_self(h))
+        def _():
+            mir[x // 2] = x_ref[:, h * 256 : (h + 1) * 256]
 
     for rows in range(2):
         for way in range(2):
@@ -211,7 +228,6 @@
             own[yl % 2] = x_ref[:, h * 256 : (h + 1) * 256]
 
     gz[z] = x_ref[...]
-    lend(z)
 
     def y_copy(y):
         return remote(
@@ -222,41 +238,68 @@
         return remote(
             sig.at[y, part_at],
             sig.at[y, part_at],
-            x_send.at[y, d - 1],
-            x_recv.at[y, d - 1],
+            x_send.at[y, d // 2],
+            x_recv.at[y, d // 2],
             at(yl, z, yh, (x + d) % 4, k),
         )
 
+    def behind(d):
+        return part_of((x + 4 - d) % 4)
+
     def x_arrival(y, d):
-        j = 2 * ((x + 4 - d) % 4) + k
-        return remote(
-            sig.at[y, j], sig.at[y, j], x_send.at[y, d - 1], x_recv.at[y, d - 1], up
-        )
+        j = behind(d)
+        return remote(
+            sig.at[y, j], sig.at[y, j], x_send.at[y, 0], x_recv.at[y, d // 2], up
+        )
+
+    def h_copy(y, d):
+        rows = pl.ds((d // 2) * 128, 128)
+        block = sig.at[y, behind(d), rows]
+        return remote(
+            block,
+            block,
+            h_send.at[y, d // 2],
+            h_recv.at[y, d // 2],
+            at(yl, z, yh, (x + d) % 4, k),
+        )
+
+    def h_arrival(y, d):
+        block = sig.at[y, behind(2), pl.ds((d // 2) * 128, 128)]
+        return remote(block, block, h_send.at[y, 0], h_recv.at[y, d // 2], up)
 
     def k_copy(y, d):
-        j = 2 * ((x + 4 - d) % 4) + k
-        return remote(
-            sig.at[y, j], sig.at[y, j], k_send.at[y, d], k_recv.at[y, d], other
-        )
+        block = sig.at[y, behind(d)]
+        return remote(block, block, k_send.at[y, d], k_recv.at[y, d], other)
 
     def k_arrival(y, d):
-        j = 2 * ((x + 4 - d) % 4) + 1 - k
-        return remote(
-            sig.at[y, j], sig.at[y, j], k_send.at[y, d], k_recv.at[y, d], other
-        )
+        block = sig.at[y, behind(d) + 1 - 2 * k]
+        return remote(block, block, k_send.at[y, d], k_recv.at[y, d], other)
 
     def spread(y):
-        for d in (1, 3, 2):
+        for d in (1, 3):
             x_copy(y, d).start()
         k_copy(y, 0).start()
 
+    def pass_on(y, d):
+        @pl.when(y >= yl)
+        def _():
+            x_arrival(y, d).wait_recv()
+            h_copy(y, d).start()
+            k_copy(y, d).start()
+
     def near(i):
         return 2 * yh + 1 - i
 
     def far(i):
         return 3 - 2 * yh - i
 
+    late = (yh == 0) & (yl < 2)
+
+    def early(i):
+        return jnp.logical_not(late & (near(i) == yl))
+
     def make(i):
+        i_near = i
         s = 1 - i
         y = near(i)
 
@@ -281,7 +324,10 @@
                 keep = later <= first + i
                 sig[y, part_at, rows, :] = jnp.where(keep, value, 0.0).astype(BF)
             y_copy(y).start()
-            spread(y)
+
+            @pl.when(early(i_near))
+            def _():
+                spread(y)
 
     def hand_on(i):
         y = far(i)
@@ -294,17 +340,20 @@
     def swap(y):
         @pl.when(y >= yl)
         def _():
-            for d in (1, 3, 2):
-                x_arrival(y, d).wait_recv()
-                k_copy(y, d).start()
+            for d in (1, 3):
+                h_arrival(y, d).wait_recv()
+            k_copy(y, 2).start()
 
     def c_copy(y):
+        to, slot = y, yl
+        if y == 2:
+            to, slot = jnp.where(yl == 0, 1, 2), 1
         return remote(
             part.at[y - 1],
-            cin.at[yl],
+            cin.at[slot],
             c_send.at[y - 1],
-            c_recv.at[yl],
-            at(y, z, yh, x, k),
+            c_recv.at[slot],
+            at(to, z, yh, x, k),
         )
 
     def c_arrival(q):
@@ -313,63 +362,63 @@
     def product(y):
         @pl.when(y >= yl)
         def _():
+            swap(y)
             for d in range(4):
                 k_arrival(y, d).wait_recv()
             total = jnp.zeros((256, 512), F32)
             for j in range(8):
                 total += jnp.dot(sig[y, j], gz[j], preferred_element_type=F32)
 
-            @pl.when(y > yl)
+            @pl.when((y > yl) & ((y != 2) | (yl != 1)))
             def _():
                 part[y - 1] = total.astype(BF)
                 c_copy(y).start()
 
+            @pl.when((y == 2) & (yl == 1))
+            def _():
+                held[...] = total
+
             @pl.when(y == yl)
             def _():
                 acc[...] = total
 
-    gap = (part_at - z + 8) % 8
-    gap = jnp.minimum(gap, 8 - gap)
-
-    for step in range(1, 5):
-        if step < 4:
-            g_pass(step)
-            lend((z - step + 8) % 8)
-            lend((z + step) % 8)
-        else:
-            for way in range(2):
-                g_arrival(way, 3, way).wait_recv()
-            lend((z + 4) % 8)
-        if step > 1:
-
-            @pl.when(jnp.maximum(gap, 1) == step - 1)
-            def _():
-                hand_on(0)
-                hand_on(1)
-
-        @pl.when(jnp.maximum(gap, 1) == step)
-        def _():
-            make(0)
-            make(1)
-
-    swap(near(0))
-    swap(near(1))
-
-    @pl.when(gap == 4)
-    def _():
-        hand_on(0)
-        hand_on(1)
-
-    product(near(0))
-    product(near(1))
-    swap(far(0))
-    product(far(0))
-    swap(far(1))
-    product(far(1))
+    def pass_both(y, flag):
+        @pl.when(flag)
+        def _():
+            pass_on(y, 1)
+            pass_on(y, 3)
+
+    make(0)
+    make(1)
+    g_pass(1)
+    pass_both(near(0), early(0))
+    hand_on(0)
+    g_pass(2)
+    pass_both(near(1), early(1))
+    hand_on(1)
+
+    @pl.when(late)
+    def _():
+        spread(yl)
+
+    pass_both(far(0), True)
+    g_pass(3)
+    pass_both(far(1), True)
+    pass_both(yl, late)
+    for way in range(2):
+        g_arrival(way, 3, way).wait_recv()
+    for y in (3, 2, 1, 0):
+        product(y)
+
+    @pl.when(yl == 1)
+    def _():
+        c_arrival(1).wait_recv()
+        part[1] = (held[...] + cin[1].astype(F32)).astype(BF)
+        c_copy(2).start()
 
     for q in range(3):
 
-        @pl.when(q < yl)
+        @pl.when(adds(q))
         def _():
             c_arrival(q).wait_recv()
             acc[...] += cin[q].astype(F32)
@@ -443,11 +492,11 @@
         def _():
             piece_copy(h).wait_send()
 
-    for b in range(8):
-
-        @pl.when(lends & (b != part_at))
-        def _():
-            mirror_copy(b).wait_send()
+    for h in range(2):
+
+        @pl.when(gives_mirror & jnp.logical_not(mirror_self(h)))
+        def _():
+            mirror_copy(h).wait_send()
 
     for step in range(4):
         for way in range(2):
@@ -464,8 +513,9 @@
 
         @pl.when(y >= yl)
         def _():
-            for d in (1, 2, 3):
+            for d in (1, 3):
                 x_copy(y, d).wait_send()
+                h_copy(y, d).wait_send()
             for d in range(4):
                 k_copy(y, d).wait_send()
 
@@ -501,19 +551,22 @@
             pltpu.VMEM((3, high, wide), BF),
             pltpu.VMEM((3, high, wide), BF),
             pltpu.VMEM((high, wide), F32),
+            pltpu.VMEM((high, wide), F32),
             pltpu.VMEM((256, 128), F32),
             pltpu.VMEM((256, 128), F32),
             pltpu.VMEM((8, 128), F32),
             dma((2, 4, 2)),
             dma((2, 4, 2)),
-            dma((8,)),
+            dma((2,)),
             dma((2,)),
             dma((2,)),
             dma((2,)),
             dma((4,)),
             dma((4,)),
-            dma((4, 3)),
-            dma((4, 3)),
+            dma((4, 2)),
+            dma((4, 2)),
+            dma((4, 2)),
+            dma((4, 2)),
             dma((4, 4)),
             dma((4, 4)),
             dma((3,)),

time: 101 us -> 83.1 us (0.82)
  the two profiles are of different devices: /device:TPU:22 before, /device:TPU:8 now
where the time goes in v4:
time: 83.1 us; the launch traced here: 82.9 us
  Pallas kernels  77.3 us (93%)
  local copies, waits for them, and re-layouts  4.86 us (6%)
    pallas_call x1, Pallas kernels, shards(): pl.pallas_call(kernel, out_shape=(jax.ShapeDtypeStruct((high, wide), BF),...  77.3 us
    reshape x2, local copies, waits for them, and re-layouts, shards(): green.reshape(rows, cols, orbit, orbit)  1.82 us

profile of v4, /device:TPU:8, one launch (start us, length us, event | category | flops | bytes accessed | tf_op | source)
XLA Modules:
  0.0 82.9 jit_solution(11476202147397993527)
XLA Ops:
  0.6 1.5 %reshape.23 = bf16[4,8,64,64]{3,2,1,0:T(8,128)(2,1)S(1)} reshape(bf16[4,8,4096]{2,1,0:T(8,128)(2,1)} %param.2) | data formatting | bytes 524288 | tf_op jit(solution)/shard_map/reshape | solution.py:533
  2.1 0.3 copy.8
  2.5 0.0 copy-start
  2.5 0.3 reshape.24.x_ref
  2.8 0.3 copy-done
  3.1 0.1 mul.16
  3.2 0.1 broadcast_multiply_fusion.pair_ref
  3.3 77.3 %collide.1 = (bf16[256,512]{1,0:T(8,128)(2,1)S(1)}, f32[8,128]{1,0:T(8,128)S(1)}) custom-call(bf16[256,512]{1,0:T(8,128)(2,1)S(1)} %reshape.24.x_ref, f32[64,512]{1,0:T(8,128)S(1)} %broadcast_multiply_fusion.pair_ref), custom_call_target="tpu_custom_call" | custom-call | flops 2147483648 | bytes 524288 | tf_op jit(solution)/shard_map/collide/pallas_call | solution.py:538
  80.6 0.3 reshape.25
  80.9 0.1 copy.5
  81.0 1.2 %reshape.26 = bf16[4,8,4096]{2,1,0:T(8,128)(2,1)} reshape(bf16[4,8,64,64]{3,2,1,0:T(8,128)(2,1)S(1)} %copy.5) | data formatting | bytes 524288 | tf_op jit(solution)/shard_map/reshape | solution.py:588
  82.2 0.1 convert_element_type.13
  82.3 0.7 convert_element_type.15
  (3 shorter events, 0.0 us)
Async XLA Ops:
  2.5 0.7 copy-start

commit v5 on v4

--- a/solution.py
+++ b/solution.py
@@ -13,7 +13,7 @@
 
 def kernel(
     x_ref,
-    pair_ref,
+    coupling_ref,
     out_ref,
     new_ref,
     gz,
@@ -22,6 +22,7 @@
     sig,
     part,
     cin,
+    relay,
     acc,
     held,
     row_mid,
@@ -43,6 +44,10 @@
     k_recv,
     c_send,
     c_recv,
+    r_send,
+    r_recv,
+    q_send,
+    q_recv,
     f_send,
     f_recv,
     n_send,
@@ -107,7 +112,7 @@
         return mine & (yl // 2 == yh)
 
     def adds(q):
-        return (q < yl) & ((yl != 2) | (q == 1))
+        return (q < yl) & ((yl == 1) | (q != 0))
 
     def one(flag):
         return jnp.where(flag, 1, 0)
@@ -120,7 +125,7 @@
     greet(up)
     greet(down)
     greet(other)
-    for d in (1, 3):
+    for d in (1, 2, 3):
         greet(at(yl, z, yh, (x + d) % 4, k))
     for s in range(2):
 
@@ -142,6 +147,14 @@
         def _():
             greet(at(q, z, yh, x, k))
 
+    @pl.when(yl == 1)
+    def _():
+        greet(at(0, z, 1 - yh, x, k))
+
+    @pl.when(yl == 3)
+    def _():
+        greet(at(1, z, 1 - yh, x, k))
+
     @pl.when(z != 7)
     def _():
         greet(at(yl, 7, yh, x, k))
@@ -150,7 +163,7 @@
     def _():
         greet((31, c))
 
-    peers = 5 + jnp.minimum(3 - yl, 2) + jnp.where(z == 7, 7, 0) + jnp.where(r == 31, 3, 0)
+    peers = 6 + jnp.minimum(3 - yl, 2) + one(yl == 1) + jnp.where(z == 7, 7, 0) + jnp.where(r == 31, 3, 0)
     peers += one(2 * yh + 1 >= yl)
     for h in range(2):
         peers += one(gives_mirror & jnp.logical_not(mirror_self(h)))
@@ -243,6 +256,21 @@
             at(yl, z, yh, (x + d) % 4, k),
         )
 
+    def two_copy(y):
+        return remote(
+            sig.at[y, part_at],
+            sig.at[y, part_at],
+            h_send.at[y, 0],
+            h_recv.at[y, 0],
+            at(yl, z, yh, (x + 2) % 4, k),
+        )
+
+    def two_arrival(y):
+        j = behind(2)
+        return remote(
+            sig.at[y, j], sig.at[y, j], h_send.at[y, 0], h_recv.at[y, 0], up
+        )
+
     def behind(d):
         return part_of((x + 4 - d) % 4)
 
@@ -298,6 +326,14 @@
     def early(i):
         return jnp.logical_not(late & (near(i) == yl))
 
+    strength = coupling_ref[...]
+    square = jnp.broadcast_to(strength, (64, 64))
+    diagonal = lax.broadcasted_iota(jnp.int32, (64, 64), 0) == lax.broadcasted_iota(
+        jnp.int32, (64, 64), 1
+    )
+    column = jnp.sum(jnp.where(diagonal, square, 0.0), axis=1, keepdims=True)
+    pair = column * jnp.concatenate([strength] * 4, axis=1)
+
     def make(i):
         i_near = i
         s = 1 - i
@@ -314,7 +350,6 @@
                 piece_arrival(s).wait_recv()
 
             partner = mir[s].T
-            pair = pair_ref[:, 0:256]
             later = lax.broadcasted_iota(jnp.int32, (64, 256), 1) // 64
             first = 32 * (y - yl) + 4 * z - 4 * part_at
             for i in range(4):
@@ -336,12 +371,22 @@
         def _():
             y_copy(y).wait_recv()
             spread(y)
+            two_copy(y).start()
 
     def swap(y):
-        @pl.when(y >= yl)
+        @pl.when((y >= yl) & (y // 2 == yh))
         def _():
             for d in (1, 3):
                 h_arrival(y, d).wait_recv()
+            k_copy(y, 2).start()
+
+    def collect(y):
+        @pl.when(y >= yl)
+        def _():
+            for d in (1, 3):
+                x_arrival(y, d).wait_recv()
+                k_copy(y, d).start()
+            two_arrival(y).wait_recv()
             k_copy(y, 2).start()
 
     def c_copy(y):
@@ -354,6 +399,26 @@
             c_send.at[y - 1],
             c_recv.at[slot],
             at(to, z, yh, x, k),
+        )
+
+    def round_copy(i):
+        rows = pl.ds(i * 128, 128)
+        return remote(
+            part.at[2, rows],
+            relay.at[rows],
+            r_send.at[i],
+            r_recv.at[i],
+            at(1, z, 1 - yh, x, k),
+        )
+
+    def round_pass(i):
+        rows = pl.ds(i * 128, 128)
+        return remote(
+            relay.at[rows],
+            cin.at[0, rows],
+            q_send.at[i],
+            q_recv.at[i],
+            at(3, z, 1 - yh, x, k),
         )
 
     def c_arrival(q):
@@ -372,7 +437,18 @@
             @pl.when((y > yl) & ((y != 2) | (yl != 1)))
             def _():
                 part[y - 1] = total.astype(BF)
-                c_copy(y).start()
+                if y < 3:
+                    c_copy(y).start()
+                else:
+
+                    @pl.when(yl != 0)
+                    def _():
+                        c_copy(y).start()
+
+                    @pl.when(yl == 0)
+                    def _():
+                        for i in range(2):
+                            round_copy(i).start()
 
             @pl.when((y == 2) & (yl == 1))
             def _():
@@ -401,17 +477,24 @@
     def _():
         spread(yl)
 
-    pass_both(far(0), True)
     g_pass(3)
-    pass_both(far(1), True)
-    pass_both(yl, late)
     for way in range(2):
         g_arrival(way, 3, way).wait_recv()
     for y in (3, 2, 1, 0):
+
+        @pl.when(y // 2 != yh)
+        def _():
+            collect(y)
+
+        if y == 1:
+            pass_both(yl, late)
         product(y)
 
     @pl.when(yl == 1)
     def _():
+        for i in range(2):
+            round_copy(i).wait_recv()
+            round_pass(i).start()
         c_arrival(1).wait_recv()
         part[1] = (held[...] + cin[1].astype(F32)).astype(BF)
         c_copy(2).start()
@@ -422,6 +505,13 @@
         def _():
             c_arrival(q).wait_recv()
             acc[...] += cin[q].astype(F32)
+
+    @pl.when(yl == 3)
+    def _():
+        for i in range(2):
+            rows = slice(i * 128, (i + 1) * 128)
+            round_pass(i).wait_recv()
+            acc[rows, :] += cin[0, rows, :].astype(F32)
 
     out_ref[...] = (step_size * acc[...]).astype(BF)
 
@@ -469,7 +559,7 @@
                 other,
             ).wait_recv()
 
-        for to in range(7):
+        for to in (3, 2, 4, 1, 5, 0, 6):
             n_copy(to).start()
         row_in[...] = row_src[pl.ds(pl.multiple_of(yl * 64 + 56, 8), 8), :]
         for to in range(7):
@@ -515,15 +605,33 @@
         def _():
             for d in (1, 3):
                 x_copy(y, d).wait_send()
-                h_copy(y, d).wait_send()
+
+                @pl.when(y // 2 == yh)
+                def _():
+                    h_copy(y, d).wait_send()
+
+            @pl.when(y // 2 != yh)
+            def _():
+                two_copy(y).wait_send()
+
             for d in range(4):
                 k_copy(y, d).wait_send()
 
         if y > 0:
 
-            @pl.when(y > yl)
+            @pl.when((y > yl) & ((y != 3) | (yl != 0)))
             def _():
                 c_copy(y).wait_send()
+
+    for i in range(2):
+
+        @pl.when(yl == 0)
+        def _():
+            round_copy(i).wait_send()
+
+        @pl.when(yl == 1)
+        def _():
+            round_pass(i).wait_send()
 
 
 def shards(green, coupling):
@@ -532,7 +640,6 @@
     high, wide = rows * orbit, cols * orbit
     matrix = jnp.transpose(green.reshape(rows, cols, orbit, orbit), (0, 2, 1, 3))
     matrix = matrix.reshape(high, wide)
-    pair = coupling[:, None] * jnp.tile(coupling, cols)[None, :]
     vmem = pl.BlockSpec(memory_space=pltpu.VMEM)
     dma = pltpu.SemaphoreType.DMA
     collision, fresh = pl.pallas_call(
@@ -550,6 +657,7 @@
             pltpu.VMEM((4, 8, high, high), BF),
             pltpu.VMEM((3, high, wide), BF),
             pltpu.VMEM((3, high, wide), BF),
+            pltpu.VMEM((high, wide), BF),
             pltpu.VMEM((high, wide), F32),
             pltpu.VMEM((high, wide), F32),
             pltpu.VMEM((256, 128), F32),
@@ -571,6 +679,10 @@
             dma((4, 4)),
             dma((3,)),
             dma((3,)),
+            dma((2,)),
+            dma((2,)),
+            dma((2,)),
+            dma((2,)),
             dma((3,)),
             dma(()),
             dma((7,)),
@@ -583,7 +695,7 @@
             flops=2 * high * wide * 8192, bytes_accessed=4 * high * wide, transcendentals=0
         ),
         name="collide",
-    )(matrix, pair)
+    )(matrix, coupling.reshape(1, orbit))
     collision = collision.reshape(rows, orbit, cols, orbit).transpose(0, 2, 1, 3)
     collision = collision.reshape(rows, cols, width)
     fresh = fresh.reshape(2, 4, 2, orbit).transpose(1, 2, 0, 3).reshape(cols, 128)

time: 83.1 us -> 82.4 us (level)
  the two profiles are of different devices: /device:TPU:8 before, /device:TPU:50 now
where the time goes in v5:
time: 82.4 us; the launch traced here: 82.2 us
  Pallas kernels  76.8 us (93%)
  local copies, waits for them, and re-layouts  4.78 us (6%)
    pallas_call x1, Pallas kernels, shards(): pl.pallas_call(kernel, out_shape=(jax.ShapeDtypeStruct((high, wide), BF),...  76.8 us
    reshape x2, local copies, waits for them, and re-layouts, shards(): green.reshape(rows, cols, orbit, orbit)  1.82 us

profile of v5, /device:TPU:50, one launch (start us, length us, event | category | flops | bytes accessed | tf_op | source)
XLA Modules:
  0.0 82.2 jit_solution(11737465344035797139)
XLA Ops:
  0.6 1.5 %reshape.23 = bf16[4,8,64,64]{3,2,1,0:T(8,128)(2,1)S(1)} reshape(bf16[4,8,4096]{2,1,0:T(8,128)(2,1)} %param.2) | data formatting | bytes 524288 | tf_op jit(solution)/shard_map/reshape | solution.py:641
  2.1 0.3 copy.8
  2.5 0.0 copy-start
  2.5 0.3 reshape.24.x_ref
  2.8 0.3 copy-done
  3.1 76.8 %collide.1 = (bf16[256,512]{1,0:T(8,128)(2,1)S(1)}, f32[8,128]{1,0:T(8,128)S(1)}) custom-call(bf16[256,512]{1,0:T(8,128)(2,1)S(1)} %reshape.24.x_ref, f32[1,64]{1,0:T(1,128)S(1)} %bitcast.10), custom_call_target="tpu_custom_call" | custom-call | flops 2147483648 | bytes 524288 | tf_op jit(solution)/shard_map/collide/pallas_call | solution.py:645
  79.9 0.1 convert_element_type.13
  80.0 0.7 convert_element_type.15
  80.6 0.3 reshape.26
  80.9 0.1 copy.5
  81.1 1.2 %reshape.27 = bf16[4,8,4096]{2,1,0:T(8,128)(2,1)} reshape(bf16[4,8,64,64]{3,2,1,0:T(8,128)(2,1)S(1)} %copy.5) | data formatting | bytes 524288 | tf_op jit(solution)/shard_map/reshape | solution.py:700
  (2 shorter events, 0.0 us)
Async XLA Ops:
  2.5 0.7 copy-start

commit v6 on v5

--- a/solution.py
+++ b/solution.py
@@ -48,8 +48,6 @@
     r_recv,
     q_send,
     q_recv,
-    f_send,
-    f_recv,
     n_send,
     n_recv,
 ):
@@ -155,15 +153,13 @@
     def _():
         greet(at(1, z, 1 - yh, x, k))
 
-    @pl.when(z != 7)
-    def _():
-        greet(at(yl, 7, yh, x, k))
-
-    @pl.when((z == 7) & (yl != 3))
-    def _():
-        greet((31, c))
-
-    peers = 6 + jnp.minimum(3 - yl, 2) + one(yl == 1) + jnp.where(z == 7, 7, 0) + jnp.where(r == 31, 3, 0)
+    for q in range(4):
+
+        @pl.when((z != 7) | (yl != q))
+        def _():
+            greet(at(q, 7, yh, x, k))
+
+    peers = 6 + jnp.minimum(3 - yl, 2) + one(yl == 1) + jnp.where(z == 7, 31, 0)
     peers += one(2 * yh + 1 >= yl)
     for h in range(2):
         peers += one(gives_mirror & jnp.logical_not(mirror_self(h)))
@@ -434,6 +430,12 @@
             for j in range(8):
                 total += jnp.dot(sig[y, j], gz[j], preferred_element_type=F32)
 
+            if y == 3:
+                for q in range(4):
+                    row_mid[q * 64 : (q + 1) * 64, :] = (
+                        step_size * total[192:256, q * 128 : (q + 1) * 128]
+                    )
+
             @pl.when((y > yl) & ((y != 2) | (yl != 1)))
             def _():
                 part[y - 1] = total.astype(BF)
@@ -490,6 +492,38 @@
             pass_both(yl, late)
         product(y)
 
+    def n_copy(to):
+        return remote(
+            row_src.at[pl.ds(pl.multiple_of(to * 8, 8), 8)],
+            row_in.at[yl],
+            n_send.at[to],
+            n_recv.at[yl],
+            (to, c),
+        )
+
+    @pl.when(z == 7)
+    def _():
+        @pl.when(yl == 3)
+        def _():
+            for q in range(4):
+                row_mid[q * 64 : (q + 1) * 64, :] += x_ref[
+                    192:256, q * 128 : (q + 1) * 128
+                ].astype(F32)
+
+        for q in range(4):
+            for i in range(2):
+                row_src[pl.ds(i * 4 + q, 32, stride=8), :] = row_mid[
+                    pl.ds(q * 64 + i, 32, stride=2), :
+                ]
+
+        @pl.loop(0, 32)
+        def _(to):
+            @pl.when(to != r)
+            def _():
+                n_copy(to).start()
+
+        row_in[yl] = row_src[pl.ds(pl.multiple_of(r * 8, 8), 8), :]
+
     @pl.when(yl == 1)
     def _():
         for i in range(2):
@@ -515,66 +549,23 @@
 
     out_ref[...] = (step_size * acc[...]).astype(BF)
 
-    def far_copy(y):
-        return remote(
-            row_src.at[pl.ds(y * 64, 64)],
-            row_src.at[pl.ds(y * 64, 64)],
-            f_send.at[y],
-            f_recv,
-            at(y, 7, yh, x, k),
-        )
-
-    def n_copy(to):
-        return remote(
-            row_src.at[pl.ds(pl.multiple_of(yl * 64 + to * 8, 8), 8)],
-            row_in,
-            n_send.at[to],
-            n_recv,
-            at(yl, to, yh, x, k),
-        )
-
-    @pl.when(r == 31)
-    def _():
-        for q in range(4):
-            lanes = slice(q * 128, (q + 1) * 128)
-            row_mid[q * 64 : (q + 1) * 64, :] = (
-                x_ref[192:256, lanes].astype(F32) + step_size * acc[192:256, lanes]
-            )
-            for i in range(2):
-                row_src[pl.ds(i * 4 + q, 32, stride=8), :] = row_mid[
-                    pl.ds(q * 64 + i, 32, stride=2), :
-                ]
-        for y in range(3):
-            far_copy(y).start()
+    for q in range(4):
+
+        @pl.when((z != 7) | (yl != q))
+        def _():
+            remote(
+                row_src.at[pl.ds(0, 8)], row_in.at[q], n_send.at[0], n_recv.at[q], up
+            ).wait_recv()
+
+    new_ref[...] = (row_in[0] + row_in[1]) + (row_in[2] + row_in[3])
 
     @pl.when(z == 7)
     def _():
-        @pl.when(yl != 3)
-        def _():
-            remote(
-                row_src.at[pl.ds(0, 64)],
-                row_src.at[pl.ds(pl.multiple_of(yl * 64, 64), 64)],
-                f_send.at[0],
-                f_recv,
-                other,
-            ).wait_recv()
-
-        for to in (3, 2, 4, 1, 5, 0, 6):
-            n_copy(to).start()
-        row_in[...] = row_src[pl.ds(pl.multiple_of(yl * 64 + 56, 8), 8), :]
-        for to in range(7):
-            n_copy(to).wait_send()
-
-    @pl.when(z != 7)
-    def _():
-        n_copy(0).wait_recv()
-
-    @pl.when(r == 31)
-    def _():
-        for y in range(3):
-            far_copy(y).wait_send()
-
-    new_ref[...] = row_in[...]
+        @pl.loop(0, 32)
+        def _(to):
+            @pl.when(to != r)
+            def _():
+                n_copy(to).wait_send()
 
     for h in range(2):
 
@@ -662,7 +653,7 @@
             pltpu.VMEM((high, wide), F32),
             pltpu.VMEM((256, 128), F32),
             pltpu.VMEM((256, 128), F32),
-            pltpu.VMEM((8, 128), F32),
+            pltpu.VMEM((4, 8, 128), F32),
             dma((2, 4, 2)),
             dma((2, 4, 2)),
             dma((2,)),
@@ -683,10 +674,8 @@
             dma((2,)),
             dma((2,)),
             dma((2,)),
-            dma((3,)),
-            dma(()),
-            dma((7,)),
-            dma(()),
+            dma((32,)),
+            dma((4,)),
         ],
         compiler_params=pltpu.CompilerParams(
             collective_id=0, has_side_effects=True, vmem_limit_bytes=40 << 20

time: 82.4 us -> 76.3 us (0.926)
  the two profiles are of different devices: /device:TPU:50 before, /device:TPU:86 now
where the time goes in v6:
time: 76.3 us; the launch traced here: 76.1 us
  Pallas kernels  70.7 us (93%)
  local copies, waits for them, and re-layouts  4.78 us (6%)
    pallas_call x1, Pallas kernels, shards(): pl.pallas_call(kernel, out_shape=(jax.ShapeDtypeStruct((high, wide), BF),...  70.7 us
    reshape x2, local copies, waits for them, and re-layouts, shards(): green.reshape(rows, cols, orbit, orbit)  1.82 us

profile of v6, /device:TPU:86, one launch (start us, length us, event | category | flops | bytes accessed | tf_op | source)
XLA Modules:
  0.0 76.1 jit_solution(8012765082604471747)
XLA Ops:
  0.6 1.5 %reshape.23 = bf16[4,8,64,64]{3,2,1,0:T(8,128)(2,1)S(1)} reshape(bf16[4,8,4096]{2,1,0:T(8,128)(2,1)} %param.2) | data formatting | bytes 524288 | tf_op jit(solution)/shard_map/reshape | solution.py:632
  2.1 0.3 copy.8
  2.5 0.0 copy-start
  2.5 0.3 reshape.24.x_ref
  2.8 0.3 copy-done
  3.1 70.7 %collide.1 = (bf16[256,512]{1,0:T(8,128)(2,1)S(1)}, f32[8,128]{1,0:T(8,128)S(1)}) custom-call(bf16[256,512]{1,0:T(8,128)(2,1)S(1)} %reshape.24.x_ref, f32[1,64]{1,0:T(1,128)S(1)} %bitcast.10), custom_call_target="tpu_custom_call" | custom-call | flops 2147483648 | bytes 524288 | tf_op jit(solution)/shard_map/collide/pallas_call | solution.py:636
  73.8 0.1 convert_element_type.13
  73.9 0.7 convert_element_type.15
  74.5 0.3 reshape.26
  74.8 0.1 copy.5
  74.9 1.2 %reshape.27 = bf16[4,8,4096]{2,1,0:T(8,128)(2,1)} reshape(bf16[4,8,64,64]{3,2,1,0:T(8,128)(2,1)S(1)} %copy.5) | data formatting | bytes 524288 | tf_op jit(solution)/shard_map/reshape | solution.py:689
  (2 shorter events, 0.0 us)
Async XLA Ops:
  2.5 0.7 copy-start

commit v7 on v6

--- a/solution.py
+++ b/solution.py
@@ -12,10 +12,14 @@
 
 
 def kernel(
-    x_ref,
-    coupling_ref,
+    green_ref,
+    strength_ref,
     out_ref,
     new_ref,
+    raw,
+    coupling_ref,
+    x_ref,
+    in_sem,
     gz,
     mir,
     own,
@@ -116,6 +120,12 @@
         return jnp.where(flag, 1, 0)
 
     barrier = pltpu.get_barrier_semaphore()
+    loads = [
+        pltpu.make_async_copy(green_ref, raw, in_sem.at[0]),
+        pltpu.make_async_copy(strength_ref, coupling_ref, in_sem.at[1]),
+    ]
+    for load in loads:
+        load.start()
 
     def greet(device):
         pl.semaphore_signal(barrier, inc=1, device_id=device, device_id_type=MESH)
@@ -158,6 +168,12 @@
         @pl.when((z != 7) | (yl != q))
         def _():
             greet(at(q, 7, yh, x, k))
+
+    for load in loads:
+        load.wait()
+    for t in range(4):
+        block = raw[t].reshape(8, 64, 64).swapaxes(0, 1).reshape(64, 512)
+        x_ref[t * 64 : (t + 1) * 64, :] = block
 
     peers = 6 + jnp.minimum(3 - yl, 2) + one(yl == 1) + jnp.where(z == 7, 31, 0)
     peers += one(2 * yh + 1 >= yl)
@@ -629,8 +645,6 @@
     rows, cols, width = green.shape
     orbit = coupling.shape[0]
     high, wide = rows * orbit, cols * orbit
-    matrix = jnp.transpose(green.reshape(rows, cols, orbit, orbit), (0, 2, 1, 3))
-    matrix = matrix.reshape(high, wide)
     vmem = pl.BlockSpec(memory_space=pltpu.VMEM)
     dma = pltpu.SemaphoreType.DMA
     collision, fresh = pl.pallas_call(
@@ -639,9 +653,13 @@
             jax.ShapeDtypeStruct((high, wide), BF),
             jax.ShapeDtypeStruct((8, 128), F32),
         ),
-        in_specs=[vmem, vmem],
+        in_specs=[pl.BlockSpec(memory_space=pl.ANY)] * 2,
         out_specs=(vmem, vmem),
         scratch_shapes=[
+            pltpu.VMEM((rows, cols, width), BF),
+            pltpu.VMEM((1, orbit), F32),
+            pltpu.VMEM((high, wide), BF),
+            dma((2,)),
             pltpu.VMEM((8, high, wide), BF),
             pltpu.VMEM((2, high, high), BF),
             pltpu.VMEM((2, high, high), BF),
@@ -684,7 +702,7 @@
             flops=2 * high * wide * 8192, bytes_accessed=4 * high * wide, transcendentals=0
         ),
         name="collide",
-    )(matrix, coupling.reshape(1, orbit))
+    )(green, coupling.reshape(1, orbit))
     collision = collision.reshape(rows, orbit, cols, orbit).transpose(0, 2, 1, 3)
     collision = collision.reshape(rows, cols, width)
     fresh = fresh.reshape(2, 4, 2, orbit).transpose(1, 2, 0, 3).reshape(cols, 128)

time: 76.3 us -> 75.4 us (0.988)
  local copies, waits for them, and re-layouts: 4.78 us -> 3.91 us
    reshape x3 -> x0, local copies, waits for them, and re-layouts: 2.14 us -> none  [the longest x2 1.82 us: shards(): green.reshape(rows, cols, orbit, orbit)]
    unnamed x2 -> x4, local copies, waits for them, and re-layouts: 0.32 us -> 1.6 us
where the time goes in v7:
time: 75.4 us; the launch traced here: 75.3 us
  Pallas kernels  70.7 us (94%)
  local copies, waits for them, and re-layouts  3.91 us (5%)
    pallas_call x1, Pallas kernels, shards(): pl.pallas_call(kernel, out_shape=(jax.ShapeDtypeStruct((high, wide), BF),...  70.7 us
    unnamed x4, local copies, waits for them, and re-layouts  1.6 us

profile of v7, /device:TPU:86, one launch (start us, length us, event | category | flops | bytes accessed | tf_op | source)
XLA Modules:
  0.0 75.3 jit_solution(4666496528394477882)
XLA Ops:
  0.6 0.0 copy-start.1
  0.6 0.6 copy-done.1
  1.3 0.0 copy-start
  1.3 0.9 %copy-done = bf16[4,8,4096]{2,1,0:T(8,128)(2,1)S(1)} copy-done((bf16[4,8,4096]{2,1,0:T(8,128)(2,1)S(1)}, bf16[4,8,4096]{2,1,0:T(8,128)(2,1)}, u32[]{:S(2)}) %copy-start) | copy-done | bytes 262168
  2.2 70.7 %collide.1 = (bf16[256,512]{1,0:T(8,128)(2,1)S(1)}, f32[8,128]{1,0:T(8,128)S(1)}) custom-call(bf16[4,8,4096]{2,1,0:T(8,128)(2,1)S(1)} %copy-done, f32[1,64]{1,0:T(1,128)S(1)} %bitcast.5), custom_call_target="tpu_custom_call" | custom-call | flops 2147483648 | bytes 524288 | tf_op jit(solution)/shard_map/collide/pallas_call | solution.py:650
  73.0 0.1 convert_element_type.13
  73.0 0.7 convert_element_type.15
  73.7 0.3 reshape.18
  74.0 0.1 copy.4
  74.1 1.2 %reshape.19 = bf16[4,8,4096]{2,1,0:T(8,128)(2,1)} reshape(bf16[4,8,64,64]{3,2,1,0:T(8,128)(2,1)S(1)} %copy.4) | data formatting | bytes 524288 | tf_op jit(solution)/shard_map/reshape | solution.py:707
  (2 shorter events, 0.0 us)
Async XLA Ops:
  0.6 0.7 copy-start.1
  1.3 0.9 %copy-start = (bf16[4,8,4096]{2,1,0:T(8,128)(2,1)S(1)}, bf16[4,8,4096]{2,1,0:T(8,128)(2,1)}, u32[]{:S(2)}) copy-start(bf16[4,8,4096]{2,1,0:T(8,128)(2,1)} %green_ref.1) | copy-start | bytes 786436

commit v8 on v7

--- a/solution.py
+++ b/solution.py
@@ -439,7 +439,10 @@
     def product(y):
         @pl.when(y >= yl)
         def _():
-            swap(y)
+            @pl.when(late & (y == yl))
+            def _():
+                swap(y)
+
             for d in range(4):
                 k_arrival(y, d).wait_recv()
             total = jnp.zeros((256, 512), F32)
@@ -496,11 +499,18 @@
         spread(yl)
 
     g_pass(3)
+    for i in range(2):
+
+        @pl.when(early(i))
+        def _():
+            swap(near(i))
+
+    collect(far(0))
     for way in range(2):
         g_arrival(way, 3, way).wait_recv()
     for y in (3, 2, 1, 0):
 
-        @pl.when(y // 2 != yh)
+        @pl.when(far(1) == y)
         def _():
             collect(y)
 
@@ -696,7 +706,7 @@
             dma((4,)),
         ],
         compiler_params=pltpu.CompilerParams(
-            collective_id=0, has_side_effects=True, vmem_limit_bytes=40 << 20
+            collective_id=0, has_side_effects=True, vmem_limit_bytes=56 << 20
         ),
         cost_estimate=pl.CostEstimate(
             flops=2 * high * wide * 8192, bytes_accessed=4 * high * wide, transcendentals=0

time: 75.4 us -> 75.5 us (level)
  the two profiles are of different devices: /device:TPU:86 before, /device:TPU:25 now
where the time goes in v8:
time: 75.5 us; the launch traced here: 75.3 us
  Pallas kernels  70.6 us (94%)
  local copies, waits for them, and re-layouts  3.3 us (4%)
    pallas_call x1, Pallas kernels, shards(): pl.pallas_call(kernel, out_shape=(jax.ShapeDtypeStruct((high, wide), BF),...  70.6 us

profile of v8, /device:TPU:25, one launch (start us, length us, event | category | flops | bytes accessed | tf_op | source)
XLA Modules:
  0.0 75.3 jit_solution(3134659355172020448)
XLA Ops:
  0.6 70.6 %collide.1 = (bf16[256,512]{1,0:T(8,128)(2,1)}, f32[8,128]{1,0:T(8,128)}) custom-call(bf16[4,8,4096]{2,1,0:T(8,128)(2,1)} %green_ref.1, f32[1,64]{1,0:T(1,128)} %bitcast.7), custom_call_target="tpu_custom_call" | custom-call | flops 2147483648 | bytes 524288 | tf_op jit(solution)/shard_map/collide/pallas_call | solution.py:660
  71.3 0.7 convert_element_type.12
  72.0 0.1 convert_element_type.13
  72.0 0.7 convert_element_type.15
  72.7 1.3 %reshape.18 = bf16[4,64,8,64]{3,2,1,0:T(8,128)(2,1)S(1)} reshape(bf16[256,512]{1,0:T(8,128)(2,1)} %get-tuple-element.4) | data formatting | bytes 524288 | tf_op jit(solution)/shard_map/reshape | solution.py:716
  74.0 0.1 copy.4
  74.1 1.2 %reshape.19 = bf16[4,8,4096]{2,1,0:T(8,128)(2,1)} reshape(bf16[4,8,64,64]{3,2,1,0:T(8,128)(2,1)S(1)} %copy.4) | data formatting | bytes 524288 | tf_op jit(solution)/shard_map/reshape | solution.py:717
  (1 shorter events, 0.0 us)

commit v9 on v8

--- a/solution.py
+++ b/solution.py
@@ -48,6 +48,8 @@
     k_recv,
     c_send,
     c_recv,
+    e_send,
+    e_recv,
     r_send,
     r_recv,
     q_send,
@@ -402,15 +404,22 @@
             k_copy(y, 2).start()
 
     def c_copy(y):
-        to, slot = y, yl
-        if y == 2:
-            to, slot = jnp.where(yl == 0, 1, 2), 1
         return remote(
             part.at[y - 1],
-            cin.at[slot],
+            cin.at[yl],
             c_send.at[y - 1],
-            c_recv.at[slot],
-            at(to, z, yh, x, k),
+            c_recv.at[yl],
+            at(y, z, yh, x, k),
+        )
+
+    def half_copy(i):
+        rows = pl.ds(i * 128, 128)
+        return remote(
+            part.at[1, rows],
+            cin.at[1, rows],
+            e_send.at[i],
+            e_recv.at[i],
+            at(jnp.minimum(yl + 1, 2), z, yh, x, k),
         )
 
     def round_copy(i):
@@ -436,8 +445,8 @@
     def c_arrival(q):
         return remote(part.at[0], cin.at[q], c_send.at[0], c_recv.at[q], up)
 
-    def product(y):
-        @pl.when(y >= yl)
+    def product(y, flag=True):
+        @pl.when((y >= yl) & flag)
         def _():
             @pl.when(late & (y == yl))
             def _():
@@ -458,8 +467,11 @@
             @pl.when((y > yl) & ((y != 2) | (yl != 1)))
             def _():
                 part[y - 1] = total.astype(BF)
-                if y < 3:
+                if y == 1:
                     c_copy(y).start()
+                elif y == 2:
+                    for i in range(2):
+                        half_copy(i).start()
                 else:
 
                     @pl.when(yl != 0)
@@ -508,6 +520,8 @@
     collect(far(0))
     for way in range(2):
         g_arrival(way, 3, way).wait_recv()
+    first = (yh == 0) & (yl == 0)
+    product(1, first)
     for y in (3, 2, 1, 0):
 
         @pl.when(far(1) == y)
@@ -516,7 +530,7 @@
 
         if y == 1:
             pass_both(yl, late)
-        product(y)
+        product(y, jnp.logical_not(first) if y == 1 else True)
 
     def n_copy(to):
         return remote(
@@ -550,30 +564,46 @@
 
         row_in[yl] = row_src[pl.ds(pl.multiple_of(r * 8, 8), 8), :]
 
+    def finish(rows, *slots):
+        total = acc[rows, :]
+        for q in slots:
+            total += cin[q, rows, :].astype(F32)
+        out_ref[rows, :] = (step_size * total).astype(BF)
+
+    halves = [slice(0, 128), slice(128, 256)]
+
+    @pl.when(yl == 0)
+    def _():
+        for i in range(2):
+            finish(halves[i])
+
     @pl.when(yl == 1)
     def _():
         for i in range(2):
             round_copy(i).wait_recv()
             round_pass(i).start()
+        for i in range(2):
+            rows = halves[i]
+            half_copy(i).wait_recv()
+            part[1, rows, :] = (held[rows, :] + cin[1, rows, :].astype(F32)).astype(BF)
+            half_copy(i).start()
+        c_arrival(0).wait_recv()
+        for i in range(2):
+            finish(halves[i], 0)
+
+    @pl.when(yl == 2)
+    def _():
+        for i in range(2):
+            half_copy(i).wait_recv()
+            finish(halves[i], 1)
+
+    @pl.when(yl == 3)
+    def _():
+        c_arrival(2).wait_recv()
         c_arrival(1).wait_recv()
-        part[1] = (held[...] + cin[1].astype(F32)).astype(BF)
-        c_copy(2).start()
-
-    for q in range(3):
-
-        @pl.when(adds(q))
-        def _():
-            c_arrival(q).wait_recv()
-            acc[...] += cin[q].astype(F32)
-
-    @pl.when(yl == 3)
-    def _():
         for i in range(2):
-            rows = slice(i * 128, (i + 1) * 128)
             round_pass(i).wait_recv()
-            acc[rows, :] += cin[0, rows, :].astype(F32)
-
-    out_ref[...] = (step_size * acc[...]).astype(BF)
+            finish(halves[i], 1, 2, 0)
 
     for q in range(4):
 
@@ -636,19 +666,23 @@
 
         if y > 0:
 
-            @pl.when((y > yl) & ((y != 3) | (yl != 0)))
-            def _():
-                c_copy(y).wait_send()
+            if y != 2:
+
+                @pl.when((y > yl) & ((y != 3) | (yl != 0)))
+                def _():
+                    c_copy(y).wait_send()
 
     for i in range(2):
 
         @pl.when(yl == 0)
         def _():
             round_copy(i).wait_send()
+            half_copy(i).wait_send()
 
         @pl.when(yl == 1)
         def _():
             round_pass(i).wait_send()
+            half_copy(i).wait_send()
 
 
 def shards(green, coupling):
@@ -702,11 +736,13 @@
             dma((2,)),
             dma((2,)),
             dma((2,)),
+            dma((2,)),
+            dma((2,)),
             dma((32,)),
             dma((4,)),
         ],
         compiler_params=pltpu.CompilerParams(
-            collective_id=0, has_side_effects=True, vmem_limit_bytes=56 << 20
+            collective_id=0, has_side_effects=True, vmem_limit_bytes=54848 << 10
         ),
         cost_estimate=pl.CostEstimate(
             flops=2 * high * wide * 8192, bytes_accessed=4 * high * wide, transcendentals=0

time: 75.5 us -> 73.5 us (0.974)
  the two profiles are of different devices: /device:TPU:25 before, /device:TPU:86 now
where the time goes in v9:
time: 73.5 us; the launch traced here: 73.3 us
  Pallas kernels  69.7 us (95%)
  local copies, waits for them, and re-layouts  2.96 us (4%)
    pallas_call x1, Pallas kernels, shards(): pl.pallas_call(kernel, out_shape=(jax.ShapeDtypeStruct((high, wide), BF),...  69.7 us

profile of v9, /device:TPU:86, one launch (start us, length us, event | category | flops | bytes accessed | tf_op | source)
XLA Modules:
  0.0 73.3 jit_solution(7837601240135911848)
XLA Ops:
  0.6 0.0 copy-start
  0.6 0.6 copy-done
  1.3 69.7 %collide.1 = (bf16[256,512]{1,0:T(8,128)(2,1)S(1)}, f32[8,128]{1,0:T(8,128)S(1)}) custom-call(bf16[4,8,4096]{2,1,0:T(8,128)(2,1)} %green_ref.1, f32[1,64]{1,0:T(1,128)S(1)} %bitcast.5), custom_call_target="tpu_custom_call" | custom-call | flops 2147483648 | bytes 524288 | tf_op jit(solution)/shard_map/collide/pallas_call | solution.py:694
  71.0 0.1 convert_element_type.13
  71.1 0.7 convert_element_type.15
  71.8 0.3 reshape.18
  72.0 0.1 copy.4
  72.2 1.2 %reshape.19 = bf16[4,8,4096]{2,1,0:T(8,128)(2,1)} reshape(bf16[4,8,64,64]{3,2,1,0:T(8,128)(2,1)S(1)} %copy.4) | data formatting | bytes 524288 | tf_op jit(solution)/shard_map/reshape | solution.py:753
  (2 shorter events, 0.0 us)
Async XLA Ops:
  0.6 0.7 copy-start

commit v10 on v9

--- a/solution.py
+++ b/solution.py
@@ -173,9 +173,12 @@
 
     for load in loads:
         load.wait()
-    for t in range(4):
-        block = raw[t].reshape(8, 64, 64).swapaxes(0, 1).reshape(64, 512)
-        x_ref[t * 64 : (t + 1) * 64, :] = block
+    for t in range(0, 4, 2):
+        pair_of_times = raw[t * 8 : t * 8 + 16, :]
+        for i in range(2):
+            block = pair_of_times[i * 8 : i * 8 + 8, :].reshape(8, 64, 64)
+            first_row = (t + i) * 64
+            x_ref[first_row : first_row + 64, :] = block.swapaxes(0, 1).reshape(64, 512)
 
     peers = 6 + jnp.minimum(3 - yl, 2) + one(yl == 1) + jnp.where(z == 7, 31, 0)
     peers += one(2 * yh + 1 >= yl)
@@ -700,7 +703,7 @@
         in_specs=[pl.BlockSpec(memory_space=pl.ANY)] * 2,
         out_specs=(vmem, vmem),
         scratch_shapes=[
-            pltpu.VMEM((rows, cols, width), BF),
+            pltpu.VMEM((rows * cols, width), BF),
             pltpu.VMEM((1, orbit), F32),
             pltpu.VMEM((high, wide), BF),
             dma((2,)),
@@ -748,7 +751,7 @@
             flops=2 * high * wide * 8192, bytes_accessed=4 * high * wide, transcendentals=0
         ),
         name="collide",
-    )(green, coupling.reshape(1, orbit))
+    )(green.reshape(rows * cols, width), coupling.reshape(1, orbit))
     collision = collision.reshape(rows, orbit, cols, orbit).transpose(0, 2, 1, 3)
     collision = collision.reshape(rows, cols, width)
     fresh = fresh.reshape(2, 4, 2, orbit).transpose(1, 2, 0, 3).reshape(cols, 128)

time: 73.5 us -> 73.5 us (level)
  no operation moved by 1% of the time
where the time goes in v10:
time: 73.5 us; the launch traced here: 73.3 us
  Pallas kernels  69.7 us (95%)
  local copies, waits for them, and re-layouts  2.96 us (4%)
    pallas_call x1, Pallas kernels, shards(): pl.pallas_call(kernel, out_shape=(jax.ShapeDtypeStruct((high, wide), BF),...  69.7 us

profile of v10, /device:TPU:86, one launch (start us, length us, event | category | flops | bytes accessed | tf_op | source)
XLA Modules:
  0.0 73.3 jit_solution(4693643680981458445)
XLA Ops:
  0.6 0.0 copy-start
  0.6 0.6 copy-done
  1.3 69.7 %collide.1 = (bf16[256,512]{1,0:T(8,128)(2,1)S(1)}, f32[8,128]{1,0:T(8,128)S(1)}) custom-call(bf16[32,4096]{1,0:T(8,128)(2,1)} %bitcast.9, f32[1,64]{1,0:T(1,128)S(1)} %bitcast.6), custom_call_target="tpu_custom_call" | custom-call | flops 2147483648 | bytes 524288 | tf_op jit(solution)/shard_map/collide/pallas_call | solution.py:697
  71.0 0.1 convert_element_type.13
  71.1 0.7 convert_element_type.15
  71.8 0.3 reshape.22
  72.0 0.1 copy.4
  72.2 1.2 %reshape.23 = bf16[4,8,4096]{2,1,0:T(8,128)(2,1)} reshape(bf16[4,8,64,64]{3,2,1,0:T(8,128)(2,1)S(1)} %copy.4) | data formatting | bytes 524288 | tf_op jit(solution)/shard_map/reshape | solution.py:756
  (2 shorter events, 0.0 us)
Async XLA Ops:
  0.6 0.7 copy-start

commit v11 on v10

--- a/solution.py
+++ b/solution.py
@@ -415,8 +415,8 @@
             at(y, z, yh, x, k),
         )
 
-    def half_copy(i):
-        rows = pl.ds(i * 128, 128)
+    def quarter_copy(i):
+        rows = pl.ds(i * 64, 64)
         return remote(
             part.at[1, rows],
             cin.at[1, rows],
@@ -426,7 +426,7 @@
         )
 
     def round_copy(i):
-        rows = pl.ds(i * 128, 128)
+        rows = pl.ds(i * 64, 64)
         return remote(
             part.at[2, rows],
             relay.at[rows],
@@ -436,7 +436,7 @@
         )
 
     def round_pass(i):
-        rows = pl.ds(i * 128, 128)
+        rows = pl.ds(i * 64, 64)
         return remote(
             relay.at[rows],
             cin.at[0, rows],
@@ -473,8 +473,8 @@
                 if y == 1:
                     c_copy(y).start()
                 elif y == 2:
-                    for i in range(2):
-                        half_copy(i).start()
+                    for i in range(4):
+                        quarter_copy(i).start()
                 else:
 
                     @pl.when(yl != 0)
@@ -483,7 +483,7 @@
 
                     @pl.when(yl == 0)
                     def _():
-                        for i in range(2):
+                        for i in range(4):
                             round_copy(i).start()
 
             @pl.when((y == 2) & (yl == 1))
@@ -573,40 +573,40 @@
             total += cin[q, rows, :].astype(F32)
         out_ref[rows, :] = (step_size * total).astype(BF)
 
-    halves = [slice(0, 128), slice(128, 256)]
+    quarters = [slice(i * 64, i * 64 + 64) for i in range(4)]
 
     @pl.when(yl == 0)
     def _():
-        for i in range(2):
-            finish(halves[i])
+        for i in range(4):
+            finish(quarters[i])
 
     @pl.when(yl == 1)
     def _():
-        for i in range(2):
+        for i in range(4):
             round_copy(i).wait_recv()
             round_pass(i).start()
-        for i in range(2):
-            rows = halves[i]
-            half_copy(i).wait_recv()
+        for i in range(4):
+            rows = quarters[i]
+            quarter_copy(i).wait_recv()
             part[1, rows, :] = (held[rows, :] + cin[1, rows, :].astype(F32)).astype(BF)
-            half_copy(i).start()
+            quarter_copy(i).start()
         c_arrival(0).wait_recv()
-        for i in range(2):
-            finish(halves[i], 0)
+        for i in range(4):
+            finish(quarters[i], 0)
 
     @pl.when(yl == 2)
     def _():
-        for i in range(2):
-            half_copy(i).wait_recv()
-            finish(halves[i], 1)
+        for i in range(4):
+            quarter_copy(i).wait_recv()
+            finish(quarters[i], 1)
 
     @pl.when(yl == 3)
     def _():
         c_arrival(2).wait_recv()
         c_arrival(1).wait_recv()
-        for i in range(2):
+        for i in range(4):
             round_pass(i).wait_recv()
-            finish(halves[i], 1, 2, 0)
+            finish(quarters[i], 1, 2, 0)
 
     for q in range(4):
 
@@ -675,17 +675,17 @@
                 def _():
                     c_copy(y).wait_send()
 
-    for i in range(2):
+    for i in range(4):
 
         @pl.when(yl == 0)
         def _():
             round_copy(i).wait_send()
-            half_copy(i).wait_send()
+            quarter_copy(i).wait_send()
 
         @pl.when(yl == 1)
         def _():
             round_pass(i).wait_send()
-            half_copy(i).wait_send()
+            quarter_copy(i).wait_send()
 
 
 def shards(green, coupling):
@@ -735,12 +735,12 @@
             dma((4, 4)),
             dma((3,)),
             dma((3,)),
-            dma((2,)),
-            dma((2,)),
-            dma((2,)),
-            dma((2,)),
-            dma((2,)),
-            dma((2,)),
+            dma((4,)),
+            dma((4,)),
+            dma((4,)),
+            dma((4,)),
+            dma((4,)),
+            dma((4,)),
             dma((32,)),
             dma((4,)),
         ],

time: 73.5 us -> 73.6 us (level)
  no operation moved by 1% of the time
where the time goes in v11:
time: 73.6 us; the launch traced here: 73.4 us
  Pallas kernels  69.8 us (95%)
  local copies, waits for them, and re-layouts  2.96 us (4%)
    pallas_call x1, Pallas kernels, shards(): pl.pallas_call(kernel, out_shape=(jax.ShapeDtypeStruct((high, wide), BF),...  69.8 us

profile of v11, /device:TPU:86, one launch (start us, length us, event | category | flops | bytes accessed | tf_op | source)
XLA Modules:
  0.0 73.4 jit_solution(18199599788295747712)
XLA Ops:
  0.6 0.0 copy-start
  0.6 0.6 copy-done
  1.3 69.8 %collide.1 = (bf16[256,512]{1,0:T(8,128)(2,1)S(1)}, f32[8,128]{1,0:T(8,128)S(1)}) custom-call(bf16[32,4096]{1,0:T(8,128)(2,1)} %bitcast.9, f32[1,64]{1,0:T(1,128)S(1)} %bitcast.6), custom_call_target="tpu_custom_call" | custom-call | flops 2147483648 | bytes 524288 | tf_op jit(solution)/shard_map/collide/pallas_call | solution.py:697
  71.1 0.1 convert_element_type.13
  71.2 0.7 convert_element_type.15
  71.8 0.3 reshape.22
  72.1 0.1 copy.4
  72.2 1.2 %reshape.23 = bf16[4,8,4096]{2,1,0:T(8,128)(2,1)} reshape(bf16[4,8,64,64]{3,2,1,0:T(8,128)(2,1)S(1)} %copy.4) | data formatting | bytes 524288 | tf_op jit(solution)/shard_map/reshape | solution.py:756
  (2 shorter events, 0.0 us)
Async XLA Ops:
  0.6 0.7 copy-start
